TPU v7x, 512 devices: a whole 4x4x16 slice. The times are simulated.
512 devices in a mesh: island: 16 (over z_lo, core), shard: 32 (over z_hi, x, y).
Axes of the slice: x: 4, y: 4, z: 16 (z_hi: 2, z_lo: 8; z = z_hi * 8 + z_lo), core: 2. Of those that a mesh axis runs over, the one named last changes fastest.
Arguments:
- features: bfloat16 [16, 4096, 2304], P('island', 'shard'), may hold values from -6 to 6
- key_grads: bfloat16 [16, 4096, 1024], P('island', 'shard'), may hold values from -0.119628906 to 0.119628906
- key_weight: bfloat16 [16, 2304, 1024], P('island', 'shard'), may hold values from -0.125 to 0.125
- weight_first: float32 [16, 2304, 1024], P('island', 'shard'), may hold values from -3 to 3
- weight_second: float32 [16, 2304, 1024], P('island', 'shard'), may hold values from 0.1 to 4
- norm_gain: float32 [16, 2304], P('island'), may hold values from 0.5 to 1.5
- gain_first: float32 [16, 2304], P('island'), may hold values from -2 to 2
- gain_second: float32 [16, 2304], P('island'), may hold values from 0.05 to 2
- outer_params: float32 [4608, 1024], P('shard'), may hold values from -6 to 6
- island_params: bfloat16 [16, 4608, 1024], P('island', 'shard'), may hold values from -6 to 6
- outer_momentum: float32 [4608, 1024], P('shard', 'island'), may hold values from -3 to 3
Outputs:
- keys: bfloat16 [16, 4096, 1024], P('island', 'shard')
- new_weight: bfloat16 [16, 2304, 1024], P('island', 'shard')
- new_weight_first: float32 [16, 2304, 1024], P('island', 'shard')
- new_weight_second: float32 [16, 2304, 1024], P('island', 'shard')
- new_gain: float32 [16, 2304], P('island')
- new_gain_first: float32 [16, 2304], P('island')
- new_gain_second: float32 [16, 2304], P('island')
- new_outer: float32 [4608, 1024], P('shard')
- new_momentum: float32 [4608, 1024], P('shard', 'island')
All inputs are finite; a program needn't handle non-finite values.
Results may differ from a plain program's by a relative error of at most 0.0037.
The roundings to bfloat16 on the way count: a program that leaves them out, or rounds other values in their place, can miss the bound.
Values may be sent and summed in bfloat16 or wider, within the bound.
No kernel may reach another device: no remote copies, remote signals or barrier semaphores. Data moves between devices by JAX's collectives and lax.ppermute only.
A program may use at most 64 MiB of HBM per device.

v0:
```python
import jax
import jax.numpy as jnp
from jax import lax
from jax.sharding import PartitionSpec as P

beta_first = 0.9
beta_second = 0.95
adam_floor = 1e-08
weight_decay = 0.1
rate_weight = 0.02
rate_gain = 0.01
momentum_keep = 0.9
rate_outer = 0.7
norm_epsilon = 1e-06


def adamw(param, grad, first, second, rate):
    first_new = beta_first * first + (1.0 - beta_first) * grad
    second_new = beta_second * second + (1.0 - beta_second) * grad * grad
    update = first_new / (jnp.sqrt(second_new) + adam_floor) + weight_decay * param
    return (param - rate * update, first_new, second_new)


def local(
    features,
    key_grads,
    key_weight,
    weight_first,
    weight_second,
    norm_gain,
    gain_first,
    gain_second,
    outer_params,
    island_params,
    outer_momentum,
):
    rows = features[0].astype(jnp.float32)
    grads = key_grads[0]
    weight = key_weight[0]
    gain = norm_gain[0]
    scaled = rows * lax.rsqrt(jnp.mean(rows * rows, axis=1, keepdims=True) + norm_epsilon)
    normed = (scaled * gain).astype(jnp.bfloat16)
    piece = lax.all_gather(weight, "shard", axis=0, tiled=True)
    keys_acc = jnp.dot(normed, piece, preferred_element_type=jnp.float32)
    back = lax.dot_general(
        grads, piece, (((1,), (1,)), ((), ())), preferred_element_type=jnp.float32
    )
    partial_gain = jnp.sum(scaled * back, axis=0)
    keys = keys_acc.astype(jnp.bfloat16)
    gain_grad = lax.psum(partial_gain, "shard")
    moved = lax.all_to_all(normed, "shard", split_axis=1, concat_axis=0, tiled=True)
    weight_grad = lax.dot_general(
        moved,
        lax.all_gather(grads, "shard", axis=0, tiled=True),
        (((0,), (0,)), ((), ())),
        preferred_element_type=jnp.float32,
    )
    new_w, new_wf, new_ws = adamw(
        weight.astype(jnp.float32), weight_grad, weight_first[0], weight_second[0], rate_weight
    )
    new_g, new_gf, new_gs = adamw(gain, gain_grad, gain_first[0], gain_second[0], rate_gain)
    drift_local = outer_params - island_params[0].astype(jnp.float32)
    island_count = lax.axis_size("island")
    column_width = outer_momentum.shape[1]
    column_start = lax.axis_index("island") * column_width
    full_moment = lax.all_gather(
        outer_momentum.astype(jnp.bfloat16), "island", axis=1, tiled=True
    ).astype(outer_momentum.dtype)
    drift = lax.psum(drift_local, "island") / island_count
    new_outer = outer_params - rate_outer * (
        (1.0 + momentum_keep) * drift + momentum_keep * momentum_keep * full_moment
    )
    own_drift = lax.dynamic_slice_in_dim(drift, column_start, column_width, 1)
    new_momentum = momentum_keep * outer_momentum + own_drift
    return (
        keys[None],
        new_w.astype(jnp.bfloat16)[None],
        new_wf[None],
        new_ws[None],
        new_g[None],
        new_gf[None],
        new_gs[None],
        new_outer,
        new_momentum,
    )


def solution(mesh):
    placed = (
        P("island", "shard", None),
        P("island", "shard", None),
        P("island", "shard", None),
        P("island", "shard", None),
        P("island", "shard", None),
        P("island", None),
        P("island", None),
        P("island", None),
        P("shard", None),
        P("island", "shard", None),
        P("shard", "island"),
    )
    return jax.shard_map(
        local,
        mesh=mesh,
        in_specs=placed,
        out_specs=(
            P("island", "shard", None),
            P("island", "shard", None),
            P("island", "shard", None),
            P("island", "shard", None),
            P("island", None),
            P("island", None),
            P("island", None),
            P("shard", None),
            P("shard", "island"),
        ),
        check_vma=False,
    )
```

profile of v0, /device:TPU:32, one launch (start us, length us, event | category | flops | bytes accessed | tf_op | source)
XLA Modules:
  0.0 808.7 jit_solution(16756978334866610693)
XLA Ops:
  8.0 0.0 copy-start.2
  8.0 0.0 all-reduce.2.cloned.1.call-start
  8.1 1.2 copy.26
  9.3 0.3 copy.28
  9.6 1.1 convert_subtract_fusion
  10.7 0.0 all-reduce.2.cloned.1.call-update
  10.7 0.0 all-gather.5.cloned.1.call-start
  10.8 0.5 all-gather.5.cloned.1.call-update
  11.3 0.0 all-gather.7.cloned.1.call-start
  11.4 0.5 all-gather.7.cloned.1.call-update
  11.9 0.1 mul.152
  12.0 0.2 copy.24
  12.3 0.2 fusion.15
  12.5 0.0 copy-start.9
  12.5 0.0 copy-start.6
  12.5 1.2 multiply_convert_fusion
  13.7 19.7 %all-to-all-start = ((bf16[128,32,72]{0,2,1:T(8,128)(2,1)}), bf16[128,32,72]{0,2,1:T(8,128)(2,1)S(1)}, u32[]{:S(2)}, u32[]{:S(2)}) async-start(bf16[128,32,72]{0,2,1:T(8,128)(2,1)} %multiply_convert_fusion), calls=%async_computation | async-start | bytes 1179648 | tf_op jit(solution)/shard_map/all_to_all | solution.py:51
  33.4 0.1 multiply_reduce_fusion
  33.5 350.1 %all-reduce.2.cloned.1.call-done = f32[144,1024]{0,1:T(8,128)} async-done(((f32[144,1024]{0,1:T(8,128)}), f32[144,1024]{0,1:T(8,128)}) %all-reduce.2.cloned.1.call-update) | async-done | bytes 589840 | tf_op jit(solution)/shard_map/psum | solution.py:69
  383.6 1.5 fusion.31
  385.1 78.3 %all_gather.11 = bf16[144,1024]{0,1:T(8,128)(2,1)S(1)} all-gather(bf16[144,64]{0,1:T(8,128)(2,1)S(1)} %get-tuple-element.34), channel_id=1, replica_groups=mesh['island'=16,'shard'=32] {'island'}, dimensions={1}, use_global_device_ids=true | all-gather | bytes 313344 | tf_op jit(solution)/shard_map/all_gather | solution.py:66
  463.4 1.5 multiply_subtract_fusion
  464.9 0.0 copy-start.1
  464.9 1.1 copy.29
  466.0 4.0 fusion.9
  470.0 319.5 %psum.14 = f32[2304]{0:T(1024)S(1)} all-reduce(f32[2304]{0:T(1024)S(1)} %fusion.9), channel_id=1, replica_groups=mesh['island'=16,'shard'=32] {'shard'}, use_global_device_ids=true, to_apply=%region_2.0 | all-reduce | flops 2304 | bytes 18432 | tf_op jit(solution)/shard_map/psum | solution.py:50
  789.5 0.6 broadcast_in_dim.26
  790.1 0.6 broadcast_in_dim.28
  790.7 0.6 broadcast_in_dim.27
  791.3 3.9 fusion.16
  795.3 0.0 all-to-all-done
  795.3 6.0 fusion.30
  (21 shorter events, 0.1 us)
Async XLA Ops:
  8.0 1.3 copy-start.2
  8.0 375.6 %all-reduce.2.cloned.1.call-start = ((), (), s32[]{:S(2)}) async-start(), calls=%async_computation.1 | async-start | bytes 2097152 | tf_op jit(solution)/shard_map/psum | solution.py:69
  10.7 1.2 copy-start.7
  10.7 1.3 copy-start
  10.7 455.3 %all-gather.5.cloned.1.call-start = ((), (), s32[]{:S(2)}) async-start(), calls=%async_computation.2 | async-start | bytes 4866048 | tf_op jit(solution)/shard_map/all_gather | solution.py:43
  11.3 784.0 %all-gather.7.cloned.1.call-start = ((), (), s32[]{:S(2)}) async-start(), calls=%async_computation.3 | async-start | bytes 8650752 | tf_op jit(solution)/shard_map/all_gather | solution.py:54
  12.5 20.9 %copy-start.8 = (f32[1,2304]{1,0:T(1,128)S(1)}, f32[1,2304]{1,0:T(1,128)}, u32[]{:S(2)}) copy-start(f32[1,2304]{1,0:T(1,128)} %param.18) | copy-start | bytes 27652
  12.5 20.9 %copy-start.9 = (f32[1,2304]{1,0:T(1,128)S(1)}, f32[1,2304]{1,0:T(1,128)}, u32[]{:S(2)}) copy-start(f32[1,2304]{1,0:T(1,128)} %param.17) | copy-start | bytes 27652
  12.5 371.1 %copy-start.6 = (f32[144,64]{0,1:T(8,128)S(1)}, f32[144,64]{0,1:T(8,128)}, u32[]{:S(2)}) copy-start(f32[144,64]{0,1:T(8,128)} %param.21) | copy-start | bytes 110596
  13.7 781.5 %all-to-all-start = ((bf16[128,32,72]{0,2,1:T(8,128)(2,1)}), bf16[128,32,72]{0,2,1:T(8,128)(2,1)S(1)}, u32[]{:S(2)}, u32[]{:S(2)}) async-start(bf16[128,32,72]{0,2,1:T(8,128)(2,1)} %multiply_convert_fusion), calls=%async_computation | async-start | bytes 1179648 | tf_op jit(solution)/shard_map/all_to_all | solution.py:51
  464.9 1.1 copy-start.1
  791.3 4.0 copy-start.3
  791.3 4.0 copy-start.4
  791.3 4.0 copy-start.5
Sparse Core Ops, SparseCore 0:
  11.8 371.7 all-reduce.1
Sparse Core Ops, SparseCore 1:
  15.6 196.4 all-gather.4
  216.4 224.0 all-gather.6
where the time goes:
time: 809 us
  blocking collectives  398 us (49%)
  waiting for transfers between devices  351 us (43%)
  starting transfers between devices  19.8 us (2%)
  between operations  15.7 us (2%)
  matrix products  13.9 us (2%)
    psum x1, waiting for transfers between devices, local(): drift = lax.psum(drift_local, 'island') / island_count  350 us
    psum x1, blocking collectives, local(): gain_grad = lax.psum(partial_gain, 'shard')  319 us
    all_gather x1, blocking collectives, local(): lax.all_gather(outer_momentum.astype(jnp.bfloat16), 'island', axis=1, til...  78.3 us
    all_to_all x1, starting transfers between devices, local(): lax.all_to_all(normed, 'shard', split_axis=1, concat_axis=0, tiled=True)  19.7 us
  transfers between devices with their start and end apart: 4, of which 1 were waited for; matrix products, arithmetic and copies ran while one was open for 2% of the time, Pallas kernels for 0%

commit v1 on v0

v1 whole, which is shorter than its diff:
```python
import functools

import jax
import jax.numpy as jnp
from jax import lax
from jax.experimental import pallas as pl
from jax.experimental.pallas import tpu as pltpu
from jax.sharding import Mesh, PartitionSpec as P

beta_first = 0.9
beta_second = 0.95
adam_floor = 1e-08
weight_decay = 0.1
rate_weight = 0.02
rate_gain = 0.01
momentum_keep = 0.9
rate_outer = 0.7
norm_epsilon = 1e-06

bf16 = jnp.bfloat16
f32 = jnp.float32

ZL, CORE, ZH, NX, NY = 8, 2, 2, 4, 4
ISLAND = ("zl", "core")
SHARD = ("zh", "x", "y")
VMEM = pl.BlockSpec(memory_space=pltpu.VMEM)
SMEM = pl.BlockSpec(memory_space=pltpu.SMEM)


def call(body, out_shape, n_in, *, scalars=0, flops=0, moved=1 << 20):
    return pl.pallas_call(
        body,
        out_shape=out_shape,
        in_specs=[SMEM] * scalars + [VMEM] * n_in,
        out_specs=jax.tree.map(lambda _: VMEM, out_shape),
        compiler_params=pltpu.CompilerParams(vmem_limit_bytes=40 << 20),
        cost_estimate=pl.CostEstimate(flops=flops, bytes_accessed=moved, transcendentals=0),
    )


def adamw(param, grad, first, second, rate):
    first_new = beta_first * first + (1.0 - beta_first) * grad
    second_new = beta_second * second + (1.0 - beta_second) * grad * grad
    update = first_new / (jnp.sqrt(second_new) + adam_floor) + weight_decay * param
    return (param - rate * update, first_new, second_new)


def diff_body(place, outer, island, out, own):
    rows = outer.shape[0] // 2
    zl, core = place[0], place[1]
    low = lax.broadcasted_iota(jnp.int32, (rows, 128), 1) < 64
    for pair in range(outer.shape[1] // 128):
        cols = slice(128 * pair, 128 * pair + 128)
        delta = outer[:, cols] - island[:, cols].astype(f32)
        top, bottom = delta[:rows], delta[rows:]
        out[2 * pair] = jnp.where(low, top, pltpu.roll(bottom, 64, 1)).astype(bf16)
        out[2 * pair + 1] = jnp.where(low, pltpu.roll(top, 64, 1), bottom).astype(bf16)
    mine = outer[:, pl.ds(pl.multiple_of(zl * 128, 128), 128)]
    top, bottom = mine[:rows], mine[rows:]
    own[...] = jnp.where(
        core == 0,
        jnp.where(low, top, pltpu.roll(bottom, 64, 1)),
        jnp.where(low, pltpu.roll(top, 64, 1), bottom),
    )


def norm_body(features, grads, gain, out):
    rows = features[...].astype(f32)
    scaled = rows * lax.rsqrt(jnp.mean(rows * rows, axis=1, keepdims=True) + norm_epsilon)
    turned = jnp.transpose(scaled * gain[...])
    width = turned.shape[0] // (ZH * NX * NY)
    turned_grads = jnp.transpose(grads[...].astype(f32)).astype(bf16)
    for y in range(NY):
        parts = []
        for x in range(NX):
            for zh in range(ZH):
                at = ((zh * NX + x) * NY + y) * width
                parts.append(turned[at : at + width])
        block = jnp.concatenate(parts, axis=0).astype(bf16)
        out[y, : block.shape[0], :] = block
        out[y, block.shape[0] :, :] = turned_grads


def dw_body(got, out):
    part = out.shape[1]
    wide = NX * part
    grads = jnp.concatenate([got[s, wide:, :] for s in range(NY)], axis=1)
    for x in range(NX):
        rows = slice(x * part, (x + 1) * part)
        normed = jnp.concatenate([got[s, rows, :] for s in range(NY)], axis=1)
        out[x] = lax.dot_general(
            normed, grads, (((1,), (1,)), ((), ())), preferred_element_type=f32
        ).astype(bf16)


def keys_body(got, weight, out):
    wide = weight.shape[0]
    for s in range(NY):
        out[s] = lax.dot_general(
            got[s, :wide, :], weight[...], (((0,), (0,)), ((), ())), preferred_element_type=f32
        ).astype(bf16)


def dwsum_body(zh_ref, got, weight, gain, own, gain_own, send):
    half = own.shape[0]
    width = own.shape[1]
    low = zh_ref[0] == 0
    total = got[0].astype(f32)
    for s in range(1, NX):
        total = total + got[s].astype(f32)
    dots = jnp.sum(total * weight[...].astype(f32), axis=1, keepdims=True) / gain[...]
    own[...] = jnp.where(low, total[:half], total[half:])
    send[:, :width] = jnp.where(low, total[half:], total[:half]).astype(bf16)
    lane = lax.broadcasted_iota(jnp.int32, (half, 128), 1)
    first, second = dots[:half], dots[half:]
    gain_own[...] = jnp.where(lane == 0, first, second)
    first_hi, second_hi = first.astype(bf16).astype(f32), second.astype(bf16).astype(f32)
    packed = jnp.where(
        lane == 0,
        first_hi,
        jnp.where(lane == 1, second_hi, jnp.where(lane == 2, first - first_hi, second - second_hi)),
    )
    send[:, width:] = packed.astype(bf16)


def local(
    features,
    key_grads,
    key_weight,
    weight_first,
    weight_second,
    norm_gain,
    gain_first,
    gain_second,
    outer_params,
    island_params,
    outer_momentum,
):
    tokens, wide = features.shape[1:]
    width = key_weight.shape[2]
    part = wide // (ZH * NX * NY)
    group = wide // NY
    n_island = ZL * CORE
    rows = outer_params.shape[0]
    zh, x, y = (lax.axis_index(a) for a in SHARD)
    weight = key_weight[0]

    pair_weight = lax.all_gather(weight, "zh", axis=0, tiled=True)
    group_weight = lax.all_gather(pair_weight, "x", axis=0, tiled=True)

    place = jnp.stack([lax.axis_index("zl"), lax.axis_index("core")]).astype(jnp.int32)
    sent, own_outer = call(
        diff_body,
        (
            jax.ShapeDtypeStruct((n_island, rows // 2, 128), bf16),
            jax.ShapeDtypeStruct((rows // 2, 128), f32),
        ),
        2,
        scalars=1,
    )(place, outer_params, island_params[0])
    sent = lax.all_to_all(sent, ISLAND, 0, 0, tiled=True)
    drift = jnp.sum(sent.astype(f32), axis=0) / n_island
    moment = jnp.concatenate([outer_momentum[: rows // 2], outer_momentum[rows // 2 :]], axis=1)
    moment = momentum_keep * moment + drift
    new_momentum = jnp.concatenate([moment[:, :64], moment[:, 64:]], axis=0)
    step = own_outer - rate_outer * (drift + momentum_keep * moment)
    step = lax.all_to_all(
        jnp.broadcast_to(step.astype(bf16)[None], (n_island,) + step.shape), ISLAND, 0, 0, tiled=True
    )
    step = step.reshape(n_island, rows // 2, 2, 64).transpose(2, 1, 0, 3).reshape(rows, width)
    new_outer = step.astype(f32)

    got = call(norm_body, jax.ShapeDtypeStruct((NY, group + width, tokens), bf16), 3)(
        features[0], key_grads[0], norm_gain
    )
    got = lax.all_to_all(got, "y", 0, 0, tiled=True)
    partial = call(
        dw_body, jax.ShapeDtypeStruct((NX, ZH * part, width), bf16), 1, flops=2 * group * width * tokens * NY
    )(got)
    partial = lax.all_to_all(partial, "x", 0, 0, tiled=True)
    gain_pair = lax.dynamic_index_in_dim(
        norm_gain.reshape(ZH, NX * NY, part), x * NY + y, 1, keepdims=False
    )
    own, gain_own, send = call(
        dwsum_body,
        (
            jax.ShapeDtypeStruct((part, width), f32),
            jax.ShapeDtypeStruct((part, 128), f32),
            jax.ShapeDtypeStruct((part, width + 128), bf16),
        ),
        3,
        scalars=1,
    )(zh.astype(jnp.int32)[None], partial, pair_weight, gain_pair.reshape(ZH * part, 1))
    both = lax.all_gather(send, "zh", axis=0, tiled=False)
    other = lax.dynamic_index_in_dim(both, 1 - zh, 0, keepdims=False).astype(f32)
    weight_grad = own + other[:, :width]
    new_w, new_wf, new_ws = adamw(
        weight.astype(f32), weight_grad, weight_first[0], weight_second[0], rate_weight
    )

    keys = call(
        keys_body,
        jax.ShapeDtypeStruct((NY, tokens, width), bf16),
        2,
        flops=2 * group * width * tokens * NY,
    )(got, group_weight)
    keys = lax.all_to_all(keys, "y", 0, 0, tiled=True)
    keys = jnp.sum(keys.astype(f32), axis=0).astype(bf16)

    gain_sum = gain_own[:, :2] + (other[:, width : width + 2] + other[:, width + 2 : width + 4])
    tile = jnp.pad(gain_sum.T, ((0, 8 - ZH), (0, 128 - part)))
    tiles = lax.all_to_all(
        jnp.broadcast_to(tile[None], (NX * NY,) + tile.shape), ("x", "y"), 0, 0, tiled=True
    )
    gain_grad = tiles[:, :ZH, :part].transpose(1, 0, 2).reshape(1, wide)
    new_g, new_gf, new_gs = adamw(norm_gain, gain_grad, gain_first, gain_second, rate_gain)
    return (
        keys[None],
        new_w.astype(bf16)[None],
        new_wf[None],
        new_ws[None],
        new_g,
        new_gf,
        new_gs,
        new_outer,
        new_momentum,
    )


def solution(mesh):
    grid = Mesh(mesh.devices.reshape(ZL, CORE, ZH, NX, NY), ISLAND + SHARD)
    block = P(ISLAND, SHARD, None)
    vector = P(ISLAND, None)
    fragment = P(SHARD, None)
    momentum = P(SHARD, ISLAND)
    return jax.shard_map(
        local,
        mesh=grid,
        in_specs=(block,) * 5 + (vector,) * 3 + (fragment, block, momentum),
        out_specs=(block,) * 4 + (vector,) * 3 + (fragment, momentum),
        check_vma=False,
    )
```

time: 809 us -> 186 us (0.23)
  the two profiles are of different devices: /device:TPU:32 before, /device:TPU:1 now
where the time goes in v1:
time: 186 us; the launch traced here: 185 us
  waiting for transfers between devices  60.3 us (32%)
  starting transfers between devices  53.1 us (29%)
  blocking collectives  32.1 us (17%)
  between operations  14.3 us (8%)
  local copies, waits for them, and re-layouts  13.5 us (7%)
  Pallas kernels  6.98 us (4%)
  other arithmetic  4.89 us (3%)
    all_to_all x1, starting transfers between devices, local(): sent = lax.all_to_all(sent, ISLAND, 0, 0, tiled=True)  19.2 us
    all_gather x1, blocking collectives, local(): pair_weight = lax.all_gather(weight, 'zh', axis=0, tiled=True)  17.2 us
    all_to_all x1, starting transfers between devices, local(): lax.all_to_all(jnp.broadcast_to(step.astype(bf16)[None], (n_island,) + st...  16 us
    all_to_all x1, waiting for transfers between devices, local(): sent = lax.all_to_all(sent, ISLAND, 0, 0, tiled=True)  15.6 us
    all_gather x1, blocking collectives, local(): both = lax.all_gather(send, 'zh', axis=0, tiled=False)  15 us
    all_to_all x1, waiting for transfers between devices, local(): got = lax.all_to_all(got, 'y', 0, 0, tiled=True)  14.3 us
    all_to_all x1, waiting for transfers between devices, local(): lax.all_to_all(jnp.broadcast_to(step.astype(bf16)[None], (n_island,) + st...  13 us
    all_to_all x1, waiting for transfers between devices, local(): keys = lax.all_to_all(keys, 'y', 0, 0, tiled=True)  10.8 us
  transfers between devices with their start and end apart: 7, of which 5 were waited for; matrix products, arithmetic and copies ran while one was open for 6% of the time, Pallas kernels for 3%

profile of v1, /device:TPU:1, one launch (start us, length us, event | category | flops | bytes accessed | tf_op | source)
XLA Modules:
  0.0 185.2 jit_solution(2541928202525802358)
XLA Ops:
  7.2 1.1 copy-done.4
  8.2 0.9 copy-done.6
  9.2 0.7 copy-done.7
  9.9 1.7 shard_map.178
  11.6 5.1 %all-to-all-start = ((bf16[4,1600,128]{2,1,0:T(8,128)(2,1)}), bf16[4,1600,128]{2,1,0:T(8,128)(2,1)S(1)}, u32[]{:S(2)}, u32[]{:S(2)}) async-start(bf16[4,1600,128]{2,1,0:T(8,128)(2,1)} %shard_map.178), calls=%async_computation | async-start | bytes 3276800 | tf_op jit(solution)/shard_map/all_to_all | solution.py:176
  16.8 1.4 shard_map.182
  18.2 14.3 %all-to-all-done.got = bf16[4,1600,128]{2,1,0:T(8,128)(2,1)S(1)} async-done(((bf16[4,1600,128]{2,1,0:T(8,128)(2,1)}), bf16[4,1600,128]{2,1,0:T(8,128)(2,1)S(1)}, u32[]{:S(2)}, u32[]{:S(2)}) %all-to-all-start) | async-done | bytes 1638432 | tf_op jit(solution)/shard_map/all_to_all | solution.py:176
  32.5 19.2 %all-to-all-start.4 = ((bf16[16,72,128]{2,1,0:T(8,128)(2,1)}), bf16[16,72,128]{2,1,0:T(8,128)(2,1)S(1)}, u32[]{:S(2)}, u32[]{:S(2)}) async-start(bf16[16,72,128]{2,1,0:T(8,128)(2,1)} %get-tuple-element.18), calls=%async_computation.4 | async-start | bytes 589824 | tf_op jit(solution)/shard_map/all_to_all | solution.py:161
  51.6 1.5 shard_map.180
  53.2 1.0 copy-done
  54.2 15.6 %all-to-all-done.4 = bf16[16,72,128]{2,1,0:T(8,128)(2,1)S(1)} async-done(((bf16[16,72,128]{2,1,0:T(8,128)(2,1)}), bf16[16,72,128]{2,1,0:T(8,128)(2,1)S(1)}, u32[]{:S(2)}, u32[]{:S(2)}) %all-to-all-start.4) | async-done | bytes 294944 | tf_op jit(solution)/shard_map/all_to_all | solution.py:161
  69.8 4.0 %all-to-all-start.2 = ((bf16[4,144,1024]{2,1,0:T(8,128)(2,1)}), bf16[4,144,1024]{2,1,0:T(8,128)(2,1)S(1)}, u32[]{:S(2)}, u32[]{:S(2)}) async-start(bf16[4,144,1024]{2,1,0:T(8,128)(2,1)} %copy-done), calls=%async_computation.2 | async-start | bytes 2359296 | tf_op jit(solution)/shard_map/all_to_all | solution.py:180
  73.8 17.2 %all-gather = bf16[1,144,1024]{2,1,0:T(8,128)(2,1)} all-gather(bf16[1,72,1024]{2,1,0:T(8,128)(2,1)S(1)} %copy-done.9), channel_id=2, replica_groups=mesh['zl'=8,'core'=2,'zh'=2,'x'=4,'y'=4] {'zh'}, dimensions={1}, use_global_device_ids=true | all-gather | bytes 442368 | tf_op jit(solution)/shard_map/all_gather | solution.py:148
  91.2 0.7 fusion.13
  92.0 1.5 copy.49
  93.5 1.5 copy.48
  96.0 15.0 %all-gather.2 = bf16[144,1152]{1,0:T(8,128)(2,1)S(1)} all-gather(bf16[72,1152]{1,0:T(8,128)(2,1)S(1)} %get-tuple-element.15), channel_id=4, replica_groups=mesh['zl'=8,'core'=2,'zh'=2,'x'=4,'y'=4] {'zh'}, dimensions={0}, use_global_device_ids=true | all-gather | bytes 497664 | tf_op jit(solution)/shard_map/all_gather | solution.py:194
  111.8 4.6 %all-to-all-start.3 = ((f32[16,8,128]{2,1,0:T(8,128)}), f32[16,8,128]{2,1,0:T(8,128)S(1)}, u32[]{:S(2)}, u32[]{:S(2)}) async-start(f32[16,8,128]{2,1,0:T(8,128)} %broadcast_in_dim.32), calls=%async_computation.3 | async-start | bytes 131072 | tf_op jit(solution)/shard_map/all_to_all | solution.py:212
  116.6 6.7 %all-to-all-done.3 = f32[16,8,128]{2,1,0:T(8,128)S(1)} async-done(((f32[16,8,128]{2,1,0:T(8,128)}), f32[16,8,128]{2,1,0:T(8,128)S(1)}, u32[]{:S(2)}, u32[]{:S(2)}) %all-to-all-start.3) | async-done | bytes 65568 | tf_op jit(solution)/shard_map/all_to_all | solution.py:212
  123.3 0.8 broadcast_in_dim.33
  124.1 16.0 %all-to-all-start.5 = ((bf16[16,72,128]{2,1,0:T(8,128)(2,1)}), bf16[16,72,128]{2,1,0:T(8,128)(2,1)S(1)}, u32[]{:S(2)}, u32[]{:S(2)}) async-start(bf16[16,72,128]{2,1,0:T(8,128)(2,1)} %broadcast_in_dim.33), calls=%async_computation.5 | async-start | bytes 589824 | tf_op jit(solution)/shard_map/all_to_all | solution.py:167
  140.1 0.7 copy.46
  140.8 1.3 copy-done.2
  142.1 2.0 %shard_map.179 = bf16[4,128,1024]{2,1,0:T(8,128)(2,1)} custom-call(bf16[4,1600,128]{2,1,0:T(8,128)(2,1)S(1)} %all-to-all-done.got, bf16[576,1024]{1,0:T(8,128)(2,1)S(1)} %bitcast.47), custom_call_target="tpu_custom_call" | custom-call | flops 603979776 | bytes 1048576 | tf_op jit(solution)/shard_map/pallas_call | solution.py:201
  144.1 1.1 fusion.10
  145.2 13.0 %all-to-all-done.5 = bf16[16,72,128]{2,1,0:T(8,128)(2,1)S(1)} async-done(((bf16[16,72,128]{2,1,0:T(8,128)(2,1)}), bf16[16,72,128]{2,1,0:T(8,128)(2,1)S(1)}, u32[]{:S(2)}, u32[]{:S(2)}) %all-to-all-start.5) | async-done | bytes 294944 | tf_op jit(solution)/shard_map/all_to_all | solution.py:167
  158.2 4.2 %all-to-all-start.1 = ((bf16[4,128,1024]{2,1,0:T(8,128)(2,1)}), bf16[4,128,1024]{2,1,0:T(8,128)(2,1)}, u32[]{:S(2)}, u32[]{:S(2)}) async-start(bf16[4,128,1024]{2,1,0:T(8,128)(2,1)} %shard_map.179), calls=%async_computation.1 | async-start | bytes 2097152 | tf_op jit(solution)/shard_map/all_to_all | solution.py:207
  162.6 0.7 multiply_subtract_fusion
  163.2 0.7 reshape.83
  164.3 1.2 reshape.82
  165.4 10.8 %all-to-all-done.1 = bf16[4,128,1024]{2,1,0:T(8,128)(2,1)} async-done(((bf16[4,128,1024]{2,1,0:T(8,128)(2,1)}), bf16[4,128,1024]{2,1,0:T(8,128)(2,1)}, u32[]{:S(2)}, u32[]{:S(2)}) %all-to-all-start.1) | async-done | bytes 1048608 | tf_op jit(solution)/shard_map/all_to_all | solution.py:207
  176.2 2.2 %reduce_sum.21 = bf16[128,1024]{1,0:T(8,128)(2,1)} reduce(bf16[4,128,1024]{2,1,0:T(8,128)(2,1)} %all-to-all-done.1, bf16[]{:T(256)} %constant.23.clone.1), dimensions={0}, to_apply=%region_0.0 | reduce | flops 393216 | bytes 1310722 | tf_op jit(solution)/shard_map/reduce_sum | solution.py:208
  (56 shorter events, 3.0 us)
Async XLA Ops:
  7.2 1.1 copy-start.4
  8.2 0.9 copy-start.6
  9.2 0.7 copy-start.7
  11.6 5.2 %copy-start.3 = (f32[144,1024]{1,0:T(8,128)S(1)}, f32[144,1024]{1,0:T(8,128)}, u32[]{:S(2)}) copy-start(f32[144,1024]{1,0:T(8,128)} %outer.1) | copy-start | bytes 1769476
  11.6 5.2 %copy-start.5 = (bf16[1,144,1024]{2,1,0:T(8,128)(2,1)S(1)}, bf16[1,144,1024]{2,1,0:T(8,128)(2,1)}, u32[]{:S(2)}) copy-start(bf16[1,144,1024]{2,1,0:T(8,128)(2,1)} %param.20) | copy-start | bytes 884740
  11.6 20.9 %all-to-all-start = ((bf16[4,1600,128]{2,1,0:T(8,128)(2,1)}), bf16[4,1600,128]{2,1,0:T(8,128)(2,1)S(1)}, u32[]{:S(2)}, u32[]{:S(2)}) async-start(bf16[4,1600,128]{2,1,0:T(8,128)(2,1)} %shard_map.178), calls=%async_computation | async-start | bytes 3276800 | tf_op jit(solution)/shard_map/all_to_all | solution.py:176
  32.5 37.3 %all-to-all-start.4 = ((bf16[16,72,128]{2,1,0:T(8,128)(2,1)}), bf16[16,72,128]{2,1,0:T(8,128)(2,1)S(1)}, u32[]{:S(2)}, u32[]{:S(2)}) async-start(bf16[16,72,128]{2,1,0:T(8,128)(2,1)} %get-tuple-element.18), calls=%async_computation.4 | async-start | bytes 589824 | tf_op jit(solution)/shard_map/all_to_all | solution.py:161
  53.2 1.0 copy-start
  54.2 19.6 %copy-start.9 = (bf16[1,72,1024]{2,1,0:T(8,128)(2,1)S(1)}, bf16[1,72,1024]{2,1,0:T(8,128)(2,1)}, u32[]{:S(2)}) copy-start(bf16[1,72,1024]{2,1,0:T(8,128)(2,1)} %param.13) | copy-start | bytes 442372
  54.2 36.8 %copy-start.8 = (f32[1,2304]{1,0:T(1,128)S(1)}, f32[1,2304]{1,0:T(1,128)}, u32[]{:S(2)}) copy-start(f32[1,2304]{1,0:T(1,128)} %gain.1) | copy-start | bytes 27652
  54.2 36.9 %copy-start.16 = (f32[144,64]{0,1:T(8,128)S(1)}, f32[144,64]{0,1:T(8,128)}, u32[]{:S(2)}) copy-start(f32[144,64]{0,1:T(8,128)} %param.21) | copy-start | bytes 110596
  69.8 25.8 %all-to-all-start.2 = ((bf16[4,144,1024]{2,1,0:T(8,128)(2,1)}), bf16[4,144,1024]{2,1,0:T(8,128)(2,1)S(1)}, u32[]{:S(2)}, u32[]{:S(2)}) async-start(bf16[4,144,1024]{2,1,0:T(8,128)(2,1)} %copy-done), calls=%async_computation.2 | async-start | bytes 2359296 | tf_op jit(solution)/shard_map/all_to_all | solution.py:180
  73.8 67.0 %all-gather.5.cloned.1.call-start = ((), (), s32[]{:S(2)}) async-start(), calls=%async_computation.6 | async-start | bytes 1474560 | tf_op jit(solution)/shard_map/all_gather | solution.py:149
  91.0 4.6 %copy-start.1 = (bf16[1,144,1024]{2,1,0:T(8,128)(2,1)S(1)}, bf16[1,144,1024]{2,1,0:T(8,128)(2,1)}, u32[]{:S(2)}) copy-start(bf16[1,144,1024]{2,1,0:T(8,128)(2,1)} %all-gather) | copy-start | bytes 884740
  96.0 20.5 %copy-start.13 = (f32[72,64]{1,0:T(8,128)S(1)}, f32[72,64]{1,0:T(8,128)}, u32[]{:S(2)}) copy-start(f32[72,64]{1,0:T(8,128)} %copy.49) | copy-start | bytes 55300
  96.0 20.5 %copy-start.14 = (f32[72,64]{1,0:T(8,128)S(1)}, f32[72,64]{1,0:T(8,128)}, u32[]{:S(2)}) copy-start(f32[72,64]{1,0:T(8,128)} %copy.48) | copy-start | bytes 55300
  96.0 20.4 %copy-start.15 = (f32[72,128]{1,0:T(8,128)S(1)}, f32[72,128]{1,0:T(8,128)}, u32[]{:S(2)}) copy-start(f32[72,128]{1,0:T(8,128)} %convert_reduce_fusion) | copy-start | bytes 110596
  111.8 11.5 %all-to-all-start.3 = ((f32[16,8,128]{2,1,0:T(8,128)}), f32[16,8,128]{2,1,0:T(8,128)S(1)}, u32[]{:S(2)}, u32[]{:S(2)}) async-start(f32[16,8,128]{2,1,0:T(8,128)} %broadcast_in_dim.32), calls=%async_computation.3 | async-start | bytes 131072 | tf_op jit(solution)/shard_map/all_to_all | solution.py:212
  124.1 34.1 %all-to-all-start.5 = ((bf16[16,72,128]{2,1,0:T(8,128)(2,1)}), bf16[16,72,128]{2,1,0:T(8,128)(2,1)S(1)}, u32[]{:S(2)}, u32[]{:S(2)}) async-start(bf16[16,72,128]{2,1,0:T(8,128)(2,1)} %broadcast_in_dim.33), calls=%async_computation.5 | async-start | bytes 589824 | tf_op jit(solution)/shard_map/all_to_all | solution.py:167
  140.8 1.3 copy-start.2
  142.1 2.0 %copy-start.10 = (bf16[1,72,1024]{2,1,0:T(8,128)(2,1)S(1)}, bf16[1,72,1024]{2,1,0:T(8,128)(2,1)}, u32[]{:S(2)}) copy-start(bf16[1,72,1024]{2,1,0:T(8,128)(2,1)} %param.13) | copy-start | bytes 442372
  142.1 2.0 %copy-start.11 = (f32[1,72,1024]{2,1,0:T(8,128)S(1)}, f32[1,72,1024]{2,1,0:T(8,128)}, u32[]{:S(2)}) copy-start(f32[1,72,1024]{2,1,0:T(8,128)} %param.15) | copy-start | bytes 884740
  142.1 2.0 %copy-start.12 = (f32[1,72,1024]{2,1,0:T(8,128)S(1)}, f32[1,72,1024]{2,1,0:T(8,128)}, u32[]{:S(2)}) copy-start(f32[1,72,1024]{2,1,0:T(8,128)} %param.14) | copy-start | bytes 884740
  145.2 17.3 %copy-start.17 = (f32[1,2304]{1,0:T(1,128)S(1)}, f32[1,2304]{1,0:T(1,128)}, u32[]{:S(2)}) copy-start(f32[1,2304]{1,0:T(1,128)} %param.18) | copy-start | bytes 27652
  145.2 17.4 %copy-start.18 = (f32[1,2304]{1,0:T(1,128)S(1)}, f32[1,2304]{1,0:T(1,128)}, u32[]{:S(2)}) copy-start(f32[1,2304]{1,0:T(1,128)} %param.17) | copy-start | bytes 27652
  158.2 18.0 %all-to-all-start.1 = ((bf16[4,128,1024]{2,1,0:T(8,128)(2,1)}), bf16[4,128,1024]{2,1,0:T(8,128)(2,1)}, u32[]{:S(2)}, u32[]{:S(2)}) async-start(bf16[4,128,1024]{2,1,0:T(8,128)(2,1)} %shard_map.179), calls=%async_computation.1 | async-start | bytes 2097152 | tf_op jit(solution)/shard_map/all_to_all | solution.py:207
Sparse Core Ops, SparseCore 0:
  91.1 33.8 all-gather.4

commit v2 on v1

v2 whole, which is shorter than its diff:
```python
import functools

import jax
import jax.numpy as jnp
from jax import lax
from jax.experimental import pallas as pl
from jax.experimental.pallas import tpu as pltpu
from jax.sharding import Mesh, PartitionSpec as P

beta_first = 0.9
beta_second = 0.95
adam_floor = 1e-08
weight_decay = 0.1
rate_weight = 0.02
rate_gain = 0.01
momentum_keep = 0.9
rate_outer = 0.7
norm_epsilon = 1e-06

bf16 = jnp.bfloat16
f32 = jnp.float32

ZL, CORE, ZH, NX, NY = 8, 2, 2, 4, 4
ISLAND = ("zl", "core")
SHARD = ("zh", "x", "y")
VMEM = pl.BlockSpec(memory_space=pltpu.VMEM)
ANY = pl.BlockSpec(memory_space=pl.ANY)
SMEM = pl.BlockSpec(memory_space=pltpu.SMEM)


def call(body, out_shape, n_in, *, scalars=0, after=0, flops=0, moved=1 << 20):
    return pl.pallas_call(
        body,
        out_shape=out_shape,
        in_specs=[SMEM] * scalars + [ANY] * after + [VMEM] * n_in,
        out_specs=jax.tree.map(lambda _: VMEM, out_shape),
        compiler_params=pltpu.CompilerParams(vmem_limit_bytes=40 << 20),
        cost_estimate=pl.CostEstimate(flops=flops, bytes_accessed=moved, transcendentals=0),
    )


def adamw(param, grad, first, second, rate):
    first_new = beta_first * first + (1.0 - beta_first) * grad
    second_new = beta_second * second + (1.0 - beta_second) * grad * grad
    update = first_new / (jnp.sqrt(second_new) + adam_floor) + weight_decay * param
    return (param - rate * update, first_new, second_new)


def pack(tile, low):
    rows = tile.shape[0] // 2
    top, bottom = tile[:rows], tile[rows:]
    return (
        jnp.where(low, top, pltpu.roll(bottom, 64, 1)),
        jnp.where(low, pltpu.roll(top, 64, 1), bottom),
    )


def low_lanes(rows):
    return lax.broadcasted_iota(jnp.int32, (rows, 128), 1) < 64


def diff_body(core_ref, outer, island, mine, theirs, outer_mine):
    low = low_lanes(mine.shape[1])
    first = core_ref[0] == 0
    for pair in range(mine.shape[0]):
        cols = slice(128 * pair, 128 * pair + 128)
        whole = outer[:, cols]
        even, odd = pack(whole - island[:, cols].astype(f32), low)
        mine[pair] = jnp.where(first, even, odd)
        theirs[pair] = jnp.where(first, odd, even)
        even, odd = pack(whole, low)
        outer_mine[pair] = jnp.where(first, even, odd)


def halves_body(zh_ref, weight, weight_got, pair_weight):
    own, other = weight[...].astype(f32), weight_got[...].astype(f32)
    lower = zh_ref[0] == 0
    pair_weight[...] = jnp.concatenate(
        [jnp.where(lower, own, other), jnp.where(lower, other, own)], axis=0
    ).astype(bf16)


def norm_body(features, grads, gain, out):
    rows = features[...].astype(f32)
    scaled = rows * lax.rsqrt(jnp.mean(rows * rows, axis=1, keepdims=True) + norm_epsilon)
    turned = jnp.transpose(scaled * gain[...])
    width = turned.shape[0] // (ZH * NX * NY)
    turned_grads = jnp.transpose(grads[...].astype(f32)).astype(bf16)
    for y in range(NY):
        parts = []
        for x in range(NX):
            for zh in range(ZH):
                at = ((zh * NX + x) * NY + y) * width
                parts.append(turned[at : at + width])
        block = jnp.concatenate(parts, axis=0).astype(bf16)
        out[y, : block.shape[0], :] = block
        out[y, block.shape[0] :, :] = turned_grads


def dw_body(zl_ref, after, got, mine, theirs, moment, out, step, packed):
    del after
    part = out.shape[1]
    wide = NX * part
    grads = jnp.concatenate([got[s, wide:, :] for s in range(NY)], axis=1)
    for x in range(NX):
        rows = slice(x * part, (x + 1) * part)
        normed = jnp.concatenate([got[s, rows, :] for s in range(NY)], axis=1)
        out[x] = lax.dot_general(
            normed, grads, (((1,), (1,)), ((), ())), preferred_element_type=f32
        ).astype(bf16)
    half = packed.shape[0]
    packed[...] = jnp.concatenate([moment[:half], moment[half:]], axis=1)
    own = momentum_keep * momentum_keep * packed[...]
    for pair in range(step.shape[0]):
        drift = (mine[pair] + theirs[pair]) * ((1.0 + momentum_keep) / (ZL * CORE))
        step[pair] = jnp.where(zl_ref[0] == pair, drift + own, drift).astype(bf16)


def dwsum_body(
    zh_ref, got, weight, own, gain_own, send
):
    half = own.shape[0]
    width = own.shape[1]
    low = zh_ref[0] == 0
    total = got[0].astype(f32)
    for s in range(1, NX):
        total = total + got[s].astype(f32)
    dots = jnp.sum(total * weight[...].astype(f32), axis=1, keepdims=True)
    own[...] = jnp.where(low, total[:half], total[half:])
    send[:, :width] = jnp.where(low, total[half:], total[:half]).astype(bf16)
    lane = lax.broadcasted_iota(jnp.int32, (half, 128), 1)
    first, second = dots[:half], dots[half:]
    first_hi, second_hi = first.astype(bf16).astype(f32), second.astype(bf16).astype(f32)
    first_lo = (first - first_hi).astype(bf16).astype(f32)
    second_lo = (second - second_hi).astype(bf16).astype(f32)
    packed = jnp.where(
        lane == 0,
        first_hi,
        jnp.where(lane == 1, second_hi, jnp.where(lane == 2, first_lo, second_lo)),
    )
    gain_own[...] = packed
    send[:, width:] = packed.astype(bf16)


def keys_body(x_ref, done, got, same, before, after, across, step, step_got, out, step_out):
    del done
    part = same.shape[0]
    for s in range(NY):
        total = None
        for by, weight in ((0, same), (NX - 1, before), (1, after), (2, across)):
            source = lax.rem(x_ref[0] + by, NX)
            rows = got[s, pl.ds(pl.multiple_of(source * part, part), part), :]
            term = lax.dot_general(
                rows, weight[...], (((0,), (0,)), ((), ())), preferred_element_type=f32
            )
            total = term if total is None else total + term
        out[s] = total.astype(bf16)
    step_out[...] = (step[...].astype(f32) + step_got[...].astype(f32)).astype(bf16)


def update_body(
    zl_ref,
    own,
    got,
    weight,
    first,
    second,
    gain_own,
    step,
    step_one,
    step_two,
    step_three,
    outer_mine,
    packed,
    keys_got,
    new_w,
    new_wf,
    new_ws,
    tiles,
    outer_out,
    moment_out,
    keys,
):
    width = own.shape[1]
    grad = own[...] + got[:, :width].astype(f32)
    w, wf, ws = adamw(weight[...].astype(f32), grad, first[...], second[...], rate_weight)
    new_w[...] = w.astype(bf16)
    new_wf[...] = wf
    new_ws[...] = ws
    mine, theirs = gain_own[...], got[:, width:].astype(f32)
    total = (mine + pltpu.roll(mine, 126, 1)) + (theirs + pltpu.roll(theirs, 126, 1))
    total = jnp.concatenate([total, jnp.zeros((128 - total.shape[0], 128), f32)], axis=0)
    total = jnp.transpose(total)[:8]
    for at in range(tiles.shape[0]):
        tiles[at] = total
    half = packed.shape[0]
    mine = jnp.zeros((half, 128), f32)
    for pair in range(step.shape[0]):
        both = (step[pair].astype(f32) + step_one[pair].astype(f32)) + (
            step_two[pair].astype(f32) + step_three[pair].astype(f32)
        )
        outer_out[pair] = outer_mine[pair] - rate_outer * both
        mine = jnp.where(zl_ref[0] == pair, both, mine)
    moment = packed[...]
    drift = (mine - momentum_keep * momentum_keep * moment) * (1.0 / (1.0 + momentum_keep))
    new = momentum_keep * moment + drift
    moment_out[:half] = new[:, :64]
    moment_out[half:] = new[:, 64:]
    sums = keys_got[0].astype(f32)
    for y in range(1, NY):
        sums = sums + keys_got[y].astype(f32)
    keys[...] = sums.astype(bf16)


def join_body(core_ref, mine, got, out):
    rows = mine.shape[1]
    low = low_lanes(rows)
    first = core_ref[0] == 0
    for pair in range(mine.shape[0]):
        even = jnp.where(first, mine[pair], got[pair])
        odd = jnp.where(first, got[pair], mine[pair])
        cols = slice(128 * pair, 128 * pair + 128)
        out[:rows, cols] = jnp.where(low, even, pltpu.roll(odd, 64, 1))
        out[rows:, cols] = jnp.where(low, pltpu.roll(even, 64, 1), odd)


def swap(value, axis):
    return lax.ppermute(value, axis, [(0, 1), (1, 0)])


def shift(value, axis, by, size=4):
    return lax.ppermute(value, axis, [(i, (i + by) % size) for i in range(size)])


def ring4(value, axis):
    return value, shift(value, axis, 1), shift(value, axis, -1), shift(value, axis, 2)


def partner(value, by):
    return lax.ppermute(value, "zl", [(i, i ^ by) for i in range(ZL)])


def local(
    features,
    key_grads,
    key_weight,
    weight_first,
    weight_second,
    norm_gain,
    gain_first,
    gain_second,
    outer_params,
    island_params,
    outer_momentum,
):
    tokens, wide = features.shape[1:]
    width = key_weight.shape[2]
    part = wide // (ZH * NX * NY)
    group = wide // NY
    rows = outer_params.shape[0]
    zl, core = (lax.axis_index(a).astype(jnp.int32) for a in ISLAND)
    zh, x, y = (lax.axis_index(a).astype(jnp.int32) for a in SHARD)
    weight = key_weight[0]
    shape = jax.ShapeDtypeStruct
    half = shape((width // 128, rows // 2, 128), f32)
    half_short = shape(half.shape, bf16)

    sent = call(norm_body, shape((NY, group + width, tokens), bf16), 3)(
        features[0], key_grads[0], norm_gain
    )
    got = lax.all_to_all(sent, "y", 0, 0, tiled=True)
    pair_weight = call(halves_body, shape((ZH * part, width), bf16), 2, scalars=1)(
        zh[None], weight, swap(weight, "zh")
    )
    mine, theirs, outer_mine = call(diff_body, (half, half, half), 2, scalars=1)(
        core[None], outer_params, island_params[0]
    )
    partial, step, packed = call(
        dw_body,
        (shape((NX, ZH * part, width), bf16), half_short, shape(half.shape[1:], f32)),
        4,
        scalars=1,
        after=1,
        flops=2 * group * width * tokens * NY,
    )(zl[None], pair_weight, got, mine, swap(theirs, "core"), outer_momentum)
    partial = lax.all_to_all(partial, "x", 0, 0, tiled=True)
    group_weight = ring4(pair_weight, "x")

    own, gain_own, send = call(
        dwsum_body,
        (shape((part, width), f32), shape((part, 128), f32), shape((part, width + 128), bf16)),
        2,
        scalars=1,
    )(zh[None], partial, pair_weight)
    grad_got = swap(send, "zh")
    keys, step = call(
        keys_body,
        (shape((NY, tokens, width), bf16), half_short),
        7,
        scalars=1,
        after=1,
        flops=2 * group * width * tokens * NY,
    )(x[None], own, got, *group_weight, step, partner(step, 4))
    keys_got = lax.all_to_all(keys, "y", 0, 0, tiled=True)

    moments = shape((part, width), f32)
    new_w, new_wf, new_ws, tiles, outer_half, new_momentum, keys = call(
        update_body,
        (
            shape((part, width), bf16),
            moments,
            moments,
            shape((NX * NY, 8, 128), f32),
            half,
            shape(outer_momentum.shape, f32),
            shape((tokens, width), bf16),
        ),
        13,
        scalars=1,
    )(
        zl[None],
        own,
        grad_got,
        weight,
        weight_first[0],
        weight_second[0],
        gain_own,
        step,
        partner(step, 1),
        partner(step, 2),
        partner(step, 3),
        outer_mine,
        packed,
        keys_got,
    )
    tiles = lax.all_to_all(tiles, ("x", "y"), 0, 0, tiled=True)
    new_outer = call(join_body, shape(outer_params.shape, f32), 2, scalars=1)(
        core[None], outer_half, swap(outer_half, "core")
    )
    gain_grad = tiles[:, :ZH, :part].transpose(1, 0, 2).reshape(1, wide) / norm_gain
    new_g, new_gf, new_gs = adamw(norm_gain, gain_grad, gain_first, gain_second, rate_gain)
    return (
        keys[None],
        new_w[None],
        new_wf[None],
        new_ws[None],
        new_g,
        new_gf,
        new_gs,
        new_outer,
        new_momentum,
    )


def solution(mesh):
    grid = Mesh(mesh.devices.reshape(ZL, CORE, ZH, NX, NY), ISLAND + SHARD)
    block = P(ISLAND, SHARD, None)
    vector = P(ISLAND, None)
    fragment = P(SHARD, None)
    momentum = P(SHARD, ISLAND)
    return jax.shard_map(
        local,
        mesh=grid,
        in_specs=(block,) * 5 + (vector,) * 3 + (fragment, block, momentum),
        out_specs=(block,) * 4 + (vector,) * 3 + (fragment, momentum),
        check_vma=False,
    )
```

time: 186 us -> 142 us (0.76)
  the two profiles are of different devices: /device:TPU:1 before, /device:TPU:32 now
where the time goes in v2:
time: 142 us; the launch traced here: 141 us
  starting transfers between devices  75 us (53%)
  waiting for transfers between devices  44.7 us (31%)
  Pallas kernels  10.6 us (7%)
  local copies, waits for them, and re-layouts  8.69 us (6%)
    ppermute x4, starting transfers between devices, swap(): return lax.ppermute(value, axis, [(0, 1), (1, 0)])  30.9 us
    ppermute x4, waiting for transfers between devices, partner(): return lax.ppermute(value, 'zl', [(i, i ^ by) for i in range(ZL)])  14.3 us
    ppermute x4, waiting for transfers between devices, swap(): return lax.ppermute(value, axis, [(0, 1), (1, 0)])  13.8 us
    ppermute x4, starting transfers between devices, partner(): return lax.ppermute(value, 'zl', [(i, i ^ by) for i in range(ZL)])  13.7 us
    ppermute x3, starting transfers between devices, shift(): lax.ppermute(value, axis, [(i, (i + by) % size) for i in range(size)])  11.3 us
    ppermute x3, waiting for transfers between devices, shift(): lax.ppermute(value, axis, [(i, (i + by) % size) for i in range(size)])  9.48 us
    unnamed x42, local copies, waits for them, and re-layouts  8.58 us
    all_to_all x1, starting transfers between devices, local(): tiles = lax.all_to_all(tiles, ('x', 'y'), 0, 0, tiled=True)  5.32 us
  transfers between devices with their start and end apart: 15, of which 8 were waited for; matrix products, arithmetic and copies ran while one was open for 2% of the time, Pallas kernels for 1%

profile of v2, /device:TPU:32, one launch (start us, length us, event | category | flops | bytes accessed | tf_op | source)
XLA Modules:
  0.0 141.3 jit_solution(12250759602105500689)
XLA Ops:
  0.7 1.1 copy-done.3
  1.7 0.9 copy-done.9
  3.4 1.7 %shard_map.179 = bf16[4,1600,128]{2,1,0:T(8,128)(2,1)} custom-call(bf16[128,2304]{1,0:T(8,128)(2,1)S(1)} %bitcast.19, bf16[128,1024]{1,0:T(8,128)(2,1)S(1)} %bitcast.23, f32[1,2304]{1,0:T(1,128)S(1)} %copy-done.11), custom_call_target="tpu_custom_call" | custom-call | bytes 1048576 | tf_op jit(solution)/shard_map/pallas_call | solution.py:268
  5.1 4.6 %all-to-all-start = ((bf16[4,1600,128]{2,1,0:T(8,128)(2,1)}), bf16[4,1600,128]{2,1,0:T(8,128)(2,1)S(1)}, u32[]{:S(2)}, u32[]{:S(2)}) async-start(bf16[4,1600,128]{2,1,0:T(8,128)(2,1)} %shard_map.179), calls=%async_computation | async-start | bytes 3276800 | tf_op jit(solution)/shard_map/all_to_all | solution.py:271
  10.8 1.9 %collective-permute-start.1 = (f32[8,72,128]{2,1,0:T(8,128)S(1)}, f32[8,72,128]{2,1,0:T(8,128)S(1)}, u32[]{:S(2)}, u32[]{:S(2)}) collective-permute-start(f32[8,72,128]{2,1,0:T(8,128)S(1)} %get-tuple-element.28), channel_id=1, source_target_pairs={{0,32},{32,0},{1,33},{33,1},{2,34},{34,2},{3,35},{35,3},{4,36},{36... | collective-permute-start | bytes 884744 | tf_op jit(solution)/shard_map/ppermute | solution.py:228
  12.7 14.8 %collective-permute-start = (bf16[72,1024]{1,0:T(8,128)(2,1)S(1)}, bf16[72,1024]{1,0:T(8,128)(2,1)S(1)}, u32[]{:S(2)}, u32[]{:S(2)}) collective-permute-start(bf16[72,1024]{1,0:T(8,128)(2,1)S(1)} %bitcast.16), channel_id=1, source_target_pairs={{0,16},{16,0},{1,17},{17,1},{2,18},{18,2},{3,19},{19,3},{4,20},{20... | collective-permute-start | bytes 442376 | tf_op jit(solution)/shard_map/ppermute | solution.py:228
  27.6 13.8 %collective-permute-done.weight_got = bf16[72,1024]{1,0:T(8,128)(2,1)S(1)} collective-permute-done((bf16[72,1024]{1,0:T(8,128)(2,1)S(1)}, bf16[72,1024]{1,0:T(8,128)(2,1)S(1)}, u32[]{:S(2)}, u32[]{:S(2)}) %collective-permute-start) | collective-permute-done | bytes 147488 | tf_op jit(solution)/shard_map/ppermute | solution.py:228
  41.5 2.1 %shard_map.181 = (bf16[4,144,1024]{2,1,0:T(8,128)(2,1)S(1)}, bf16[8,72,128]{2,1,0:T(8,128)(2,1)}, f32[72,128]{1,0:T(8,128)S(1)}) custom-call(s32[1]{0:T(128)} %bitcast.zl_ref, bf16[144,1024]{1,0:T(8,128)(2,1)S(1)} %shard_map.178.after.weight.same, bf16[4,1600,128]{2,1,0:T(8,128)(2,1)S(1)} %all-to-all-done.got, f32[8,72,128]{2,1,0:T(8,128)S(1)} %get-tuple-element.27.mine, ...), custom_call_target="tpu_custom_call" | custom-call | flops 603979776 | bytes 1048576 | tf_op jit(solution)/shard_map/pallas_call | solution.py:278
  43.6 1.0 copy-done
  45.3 4.3 %all-to-all-start.1 = ((bf16[4,144,1024]{2,1,0:T(8,128)(2,1)}), bf16[4,144,1024]{2,1,0:T(8,128)(2,1)S(1)}, u32[]{:S(2)}, u32[]{:S(2)}) async-start(bf16[4,144,1024]{2,1,0:T(8,128)(2,1)} %copy-done), calls=%async_computation.1 | async-start | bytes 2359296 | tf_op jit(solution)/shard_map/all_to_all | solution.py:286
  49.6 3.9 %collective-permute-start.3 = (bf16[144,1024]{1,0:T(8,128)(2,1)S(1)}, bf16[144,1024]{1,0:T(8,128)(2,1)}, u32[]{:S(2)}, u32[]{:S(2)}) collective-permute-start(bf16[144,1024]{1,0:T(8,128)(2,1)S(1)} %shard_map.178.after.weight.same), channel_id=1, source_target_pairs={{0,4},{4,8},{8,12},{12,0},{1,5},{5,9},{9,13},{13,1},{2,6},{6,10},{... | collective-permute-start | bytes 884744 | tf_op jit(solution)/shard_map/ppermute | solution.py:232
  53.5 3.1 %collective-permute-start.4 = (bf16[144,1024]{1,0:T(8,128)(2,1)S(1)}, bf16[144,1024]{1,0:T(8,128)(2,1)}, u32[]{:S(2)}, u32[]{:S(2)}) collective-permute-start(bf16[144,1024]{1,0:T(8,128)(2,1)S(1)} %shard_map.178.after.weight.same), channel_id=1, source_target_pairs={{0,12},{4,0},{8,4},{12,8},{1,13},{5,1},{9,5},{13,9},{2,14},{6,2},{... | collective-permute-start | bytes 884744 | tf_op jit(solution)/shard_map/ppermute | solution.py:232
  56.6 4.2 %collective-permute-start.5 = (bf16[144,1024]{1,0:T(8,128)(2,1)S(1)}, bf16[144,1024]{1,0:T(8,128)(2,1)}, u32[]{:S(2)}, u32[]{:S(2)}) collective-permute-start(bf16[144,1024]{1,0:T(8,128)(2,1)S(1)} %shard_map.178.after.weight.same), channel_id=1, source_target_pairs={{0,8},{4,12},{8,0},{12,4},{1,9},{5,13},{9,1},{13,5},{2,10},{6,14},... | collective-permute-start | bytes 884744 | tf_op jit(solution)/shard_map/ppermute | solution.py:232
  60.8 4.5 %collective-permute-start.6 = (bf16[8,72,128]{2,1,0:T(8,128)(2,1)}, bf16[8,72,128]{2,1,0:T(8,128)(2,1)}, u32[]{:S(2)}, u32[]{:S(2)}) collective-permute-start(bf16[8,72,128]{2,1,0:T(8,128)(2,1)} %get-tuple-element.33.step), channel_id=1, source_target_pairs={{0,256},{64,320},{128,384},{192,448},{256,0},{320,64},{384,128},{4... | collective-permute-start | bytes 442376 | tf_op jit(solution)/shard_map/ppermute | solution.py:240
  65.4 2.2 %all-to-all-done.1.got = bf16[4,144,1024]{2,1,0:T(8,128)(2,1)S(1)} async-done(((bf16[4,144,1024]{2,1,0:T(8,128)(2,1)}), bf16[4,144,1024]{2,1,0:T(8,128)(2,1)S(1)}, u32[]{:S(2)}, u32[]{:S(2)}) %all-to-all-start.1) | async-done | bytes 1179680 | tf_op jit(solution)/shard_map/all_to_all | solution.py:286
  69.2 4.2 %collective-permute-done.3.before = bf16[144,1024]{1,0:T(8,128)(2,1)} collective-permute-done((bf16[144,1024]{1,0:T(8,128)(2,1)S(1)}, bf16[144,1024]{1,0:T(8,128)(2,1)}, u32[]{:S(2)}, u32[]{:S(2)}) %collective-permute-start.3) | collective-permute-done | bytes 294944 | tf_op jit(solution)/shard_map/ppermute | solution.py:232
  73.3 5.3 %collective-permute-done.5.across = bf16[144,1024]{1,0:T(8,128)(2,1)} collective-permute-done((bf16[144,1024]{1,0:T(8,128)(2,1)S(1)}, bf16[144,1024]{1,0:T(8,128)(2,1)}, u32[]{:S(2)}, u32[]{:S(2)}) %collective-permute-start.5) | collective-permute-done | bytes 294944 | tf_op jit(solution)/shard_map/ppermute | solution.py:232
  78.6 3.6 %shard_map.183 = (bf16[4,128,1024]{2,1,0:T(8,128)(2,1)}, bf16[8,72,128]{2,1,0:T(8,128)(2,1)S(1)}) custom-call(s32[1]{0:T(128)} %bitcast.9.x_ref, f32[72,1024]{1,0:T(8,128)S(1)} %get-tuple-element.30.done.own, bf16[4,1600,128]{2,1,0:T(8,128)(2,1)S(1)} %all-to-all-done.got, bf16[144,1024]{1,0:T(8,128)(2,1)S(1)} %shard_map.178.after.weight.same, ...), custom_call_target="tpu_custom_call" | custom-call | flops 603979776 | bytes 1048576 | tf_op jit(solution)/shard_map/pallas_call | solution.py:296
  82.2 4.9 %all-to-all-start.2 = ((bf16[4,128,1024]{2,1,0:T(8,128)(2,1)}), bf16[4,128,1024]{2,1,0:T(8,128)(2,1)S(1)}, u32[]{:S(2)}, u32[]{:S(2)}) async-start(bf16[4,128,1024]{2,1,0:T(8,128)(2,1)} %get-tuple-element.37), calls=%async_computation.2 | async-start | bytes 2097152 | tf_op jit(solution)/shard_map/all_to_all | solution.py:304
  87.2 12.2 %collective-permute-start.2 = (bf16[72,1152]{1,0:T(8,128)(2,1)S(1)}, bf16[72,1152]{1,0:T(8,128)(2,1)S(1)}, u32[]{:S(2)}, u32[]{:S(2)}) collective-permute-start(bf16[72,1152]{1,0:T(8,128)(2,1)S(1)} %copy-done.18), channel_id=1, source_target_pairs={{0,16},{16,0},{1,17},{17,1},{2,18},{18,2},{3,19},{19,3},{4,20},{20... | collective-permute-start | bytes 497672 | tf_op jit(solution)/shard_map/ppermute | solution.py:228
  99.4 1.9 %collective-permute-start.7 = (bf16[8,72,128]{2,1,0:T(8,128)(2,1)S(1)}, bf16[8,72,128]{2,1,0:T(8,128)(2,1)S(1)}, u32[]{:S(2)}, u32[]{:S(2)}) collective-permute-start(bf16[8,72,128]{2,1,0:T(8,128)(2,1)S(1)} %get-tuple-element.34.step), channel_id=1, source_target_pairs={{0,64},{64,0},{128,192},{192,128},{256,320},{320,256},{384,448},{4... | collective-permute-start | bytes 442376 | tf_op jit(solution)/shard_map/ppermute | solution.py:240
  101.3 1.9 %collective-permute-start.8 = (bf16[8,72,128]{2,1,0:T(8,128)(2,1)S(1)}, bf16[8,72,128]{2,1,0:T(8,128)(2,1)S(1)}, u32[]{:S(2)}, u32[]{:S(2)}) collective-permute-start(bf16[8,72,128]{2,1,0:T(8,128)(2,1)S(1)} %get-tuple-element.34.step), channel_id=1, source_target_pairs={{0,128},{64,192},{128,0},{192,64},{256,384},{320,448},{384,256},{4... | collective-permute-start | bytes 442376 | tf_op jit(solution)/shard_map/ppermute | solution.py:240
  103.3 5.4 %collective-permute-start.9 = (bf16[8,72,128]{2,1,0:T(8,128)(2,1)S(1)}, bf16[8,72,128]{2,1,0:T(8,128)(2,1)S(1)}, u32[]{:S(2)}, u32[]{:S(2)}) collective-permute-start(bf16[8,72,128]{2,1,0:T(8,128)(2,1)S(1)} %get-tuple-element.34.step), channel_id=1, source_target_pairs={{0,192},{64,128},{128,64},{192,0},{256,448},{320,384},{384,320},{4... | collective-permute-start | bytes 442376 | tf_op jit(solution)/shard_map/ppermute | solution.py:240
  108.6 5.7 %collective-permute-done.7.step_one = bf16[8,72,128]{2,1,0:T(8,128)(2,1)S(1)} collective-permute-done((bf16[8,72,128]{2,1,0:T(8,128)(2,1)S(1)}, bf16[8,72,128]{2,1,0:T(8,128)(2,1)S(1)}, u32[]{:S(2)}, u32[]{:S(2)}) %collective-permute-start.7) | collective-permute-done | bytes 147488 | tf_op jit(solution)/shard_map/ppermute | solution.py:240
  114.3 2.5 %collective-permute-done.8.step_two = bf16[8,72,128]{2,1,0:T(8,128)(2,1)S(1)} collective-permute-done((bf16[8,72,128]{2,1,0:T(8,128)(2,1)S(1)}, bf16[8,72,128]{2,1,0:T(8,128)(2,1)S(1)}, u32[]{:S(2)}, u32[]{:S(2)}) %collective-permute-start.8) | collective-permute-done | bytes 147488 | tf_op jit(solution)/shard_map/ppermute | solution.py:240
  116.8 6.1 %collective-permute-done.9.step_three = bf16[8,72,128]{2,1,0:T(8,128)(2,1)S(1)} collective-permute-done((bf16[8,72,128]{2,1,0:T(8,128)(2,1)S(1)}, bf16[8,72,128]{2,1,0:T(8,128)(2,1)S(1)}, u32[]{:S(2)}, u32[]{:S(2)}) %collective-permute-start.9) | collective-permute-done | bytes 147488 | tf_op jit(solution)/shard_map/ppermute | solution.py:240
  123.7 1.4 %shard_map.184 = (bf16[72,1024]{1,0:T(8,128)(2,1)}, f32[72,1024]{1,0:T(8,128)}, f32[72,1024]{1,0:T(8,128)}, f32[16,8,128]{2,1,0:T(8,128)S(1)}, f32[8,72,128]{2,1...) custom-call(s32[1]{0:T(128)} %bitcast.zl_ref, f32[72,1024]{1,0:T(8,128)S(1)} %get-tuple-element.30.done.own, ...), custom_call_target="tpu_custom_call" | custom-call | bytes 1048576 | tf_op jit(solution)/shard_map/pallas_call | solution.py:307
  125.8 5.3 %all-to-all-start.3 = ((f32[16,8,128]{2,1,0:T(8,128)}), f32[16,8,128]{2,1,0:T(8,128)S(1)}, u32[]{:S(2)}, u32[]{:S(2)}) async-start(f32[16,8,128]{2,1,0:T(8,128)} %copy-done.10), calls=%async_computation.3 | async-start | bytes 131072 | tf_op jit(solution)/shard_map/all_to_all | solution.py:336
  131.1 1.9 %collective-permute-start.10 = (f32[8,72,128]{2,1,0:T(8,128)S(1)}, f32[8,72,128]{2,1,0:T(8,128)S(1)}, u32[]{:S(2)}, u32[]{:S(2)}) collective-permute-start(f32[8,72,128]{2,1,0:T(8,128)S(1)} %get-tuple-element.43.mine), channel_id=1, source_target_pairs={{0,32},{32,0},{1,33},{33,1},{2,34},{34,2},{3,35},{35,3},{4,36},{36... | collective-permute-start | bytes 884744 | tf_op jit(solution)/shard_map/ppermute | solution.py:228
  133.7 5.0 %all-to-all-done.3 = f32[16,8,128]{2,1,0:T(8,128)S(1)} async-done(((f32[16,8,128]{2,1,0:T(8,128)}), f32[16,8,128]{2,1,0:T(8,128)S(1)}, u32[]{:S(2)}, u32[]{:S(2)}) %all-to-all-start.3) | async-done | bytes 65568 | tf_op jit(solution)/shard_map/all_to_all | solution.py:336
  138.9 1.4 multiply_subtract_fusion
  140.3 1.0 shard_map.185
  (52 shorter events, 6.4 us)
Async XLA Ops:
  0.6 1.1 copy-start.3
  1.7 0.9 copy-start.9
  2.7 0.7 copy-start.11
  5.1 4.6 %copy-start.2 = (f32[144,1024]{1,0:T(8,128)S(1)}, f32[144,1024]{1,0:T(8,128)}, u32[]{:S(2)}) copy-start(f32[144,1024]{1,0:T(8,128)} %outer.1) | copy-start | bytes 1769476
  5.1 4.6 %copy-start.8 = (bf16[1,144,1024]{2,1,0:T(8,128)(2,1)S(1)}, bf16[1,144,1024]{2,1,0:T(8,128)(2,1)}, u32[]{:S(2)}) copy-start(bf16[1,144,1024]{2,1,0:T(8,128)(2,1)} %param.20) | copy-start | bytes 884740
  5.1 7.6 %copy-start.1 = (bf16[1,72,1024]{2,1,0:T(8,128)(2,1)S(1)}, bf16[1,72,1024]{2,1,0:T(8,128)(2,1)}, u32[]{:S(2)}) copy-start(bf16[1,72,1024]{2,1,0:T(8,128)(2,1)} %param.13) | copy-start | bytes 442372
  5.1 22.5 %copy-start.19 = (f32[144,64]{0,1:T(8,128)S(1)}, f32[144,64]{0,1:T(8,128)}, u32[]{:S(2)}) copy-start(f32[144,64]{0,1:T(8,128)} %param.21) | copy-start | bytes 110596
  5.1 36.4 %all-to-all-start = ((bf16[4,1600,128]{2,1,0:T(8,128)(2,1)}), bf16[4,1600,128]{2,1,0:T(8,128)(2,1)S(1)}, u32[]{:S(2)}, u32[]{:S(2)}) async-start(bf16[4,1600,128]{2,1,0:T(8,128)(2,1)} %shard_map.179), calls=%async_computation | async-start | bytes 3276800 | tf_op jit(solution)/shard_map/all_to_all | solution.py:271
  10.1 0.7 copy-start.6
  10.8 30.7 %collective-permute-start.1 = (f32[8,72,128]{2,1,0:T(8,128)S(1)}, f32[8,72,128]{2,1,0:T(8,128)S(1)}, u32[]{:S(2)}, u32[]{:S(2)}) collective-permute-start(f32[8,72,128]{2,1,0:T(8,128)S(1)} %get-tuple-element.28), channel_id=1, source_target_pairs={{0,32},{32,0},{1,33},{33,1},{2,34},{34,2},{3,35},{35,3},{4,36},{36... | collective-permute-start | bytes 884744 | tf_op jit(solution)/shard_map/ppermute | solution.py:228
  12.7 28.7 %collective-permute-start = (bf16[72,1024]{1,0:T(8,128)(2,1)S(1)}, bf16[72,1024]{1,0:T(8,128)(2,1)S(1)}, u32[]{:S(2)}, u32[]{:S(2)}) collective-permute-start(bf16[72,1024]{1,0:T(8,128)(2,1)S(1)} %bitcast.16), channel_id=1, source_target_pairs={{0,16},{16,0},{1,17},{17,1},{2,18},{18,2},{3,19},{19,3},{4,20},{20... | collective-permute-start | bytes 442376 | tf_op jit(solution)/shard_map/ppermute | solution.py:228
  43.6 1.0 copy-start
  45.3 22.3 %all-to-all-start.1 = ((bf16[4,144,1024]{2,1,0:T(8,128)(2,1)}), bf16[4,144,1024]{2,1,0:T(8,128)(2,1)S(1)}, u32[]{:S(2)}, u32[]{:S(2)}) async-start(bf16[4,144,1024]{2,1,0:T(8,128)(2,1)} %copy-done), calls=%async_computation.1 | async-start | bytes 2359296 | tf_op jit(solution)/shard_map/all_to_all | solution.py:286
  49.6 23.8 %collective-permute-start.3 = (bf16[144,1024]{1,0:T(8,128)(2,1)S(1)}, bf16[144,1024]{1,0:T(8,128)(2,1)}, u32[]{:S(2)}, u32[]{:S(2)}) collective-permute-start(bf16[144,1024]{1,0:T(8,128)(2,1)S(1)} %shard_map.178.after.weight.same), channel_id=1, source_target_pairs={{0,4},{4,8},{8,12},{12,0},{1,5},{5,9},{9,13},{13,1},{2,6},{6,10},{... | collective-permute-start | bytes 884744 | tf_op jit(solution)/shard_map/ppermute | solution.py:232
  53.5 19.8 %collective-permute-start.4 = (bf16[144,1024]{1,0:T(8,128)(2,1)S(1)}, bf16[144,1024]{1,0:T(8,128)(2,1)}, u32[]{:S(2)}, u32[]{:S(2)}) collective-permute-start(bf16[144,1024]{1,0:T(8,128)(2,1)S(1)} %shard_map.178.after.weight.same), channel_id=1, source_target_pairs={{0,12},{4,0},{8,4},{12,8},{1,13},{5,1},{9,5},{13,9},{2,14},{6,2},{... | collective-permute-start | bytes 884744 | tf_op jit(solution)/shard_map/ppermute | solution.py:232
  56.6 22.0 %collective-permute-start.5 = (bf16[144,1024]{1,0:T(8,128)(2,1)S(1)}, bf16[144,1024]{1,0:T(8,128)(2,1)}, u32[]{:S(2)}, u32[]{:S(2)}) collective-permute-start(bf16[144,1024]{1,0:T(8,128)(2,1)S(1)} %shard_map.178.after.weight.same), channel_id=1, source_target_pairs={{0,8},{4,12},{8,0},{12,4},{1,9},{5,13},{9,1},{13,5},{2,10},{6,14},... | collective-permute-start | bytes 884744 | tf_op jit(solution)/shard_map/ppermute | solution.py:232
  60.8 17.8 %collective-permute-start.6 = (bf16[8,72,128]{2,1,0:T(8,128)(2,1)}, bf16[8,72,128]{2,1,0:T(8,128)(2,1)}, u32[]{:S(2)}, u32[]{:S(2)}) collective-permute-start(bf16[8,72,128]{2,1,0:T(8,128)(2,1)} %get-tuple-element.33.step), channel_id=1, source_target_pairs={{0,256},{64,320},{128,384},{192,448},{256,0},{320,64},{384,128},{4... | collective-permute-start | bytes 442376 | tf_op jit(solution)/shard_map/ppermute | solution.py:240
  68.5 0.7 copy-start.17
  82.2 5.0 %copy-start.18 = (bf16[72,1152]{1,0:T(8,128)(2,1)S(1)}, bf16[72,1152]{1,0:T(8,128)(2,1)}, u32[]{:S(2)}) copy-start(bf16[72,1152]{1,0:T(8,128)(2,1)} %copy-done.17) | copy-start | bytes 497668
  82.2 40.7 %copy-start.4 = (f32[1,72,1024]{2,1,0:T(8,128)S(1)}, f32[1,72,1024]{2,1,0:T(8,128)}, u32[]{:S(2)}) copy-start(f32[1,72,1024]{2,1,0:T(8,128)} %param.14) | copy-start | bytes 884740
  82.2 40.7 %copy-start.5 = (f32[1,72,1024]{2,1,0:T(8,128)S(1)}, f32[1,72,1024]{2,1,0:T(8,128)}, u32[]{:S(2)}) copy-start(f32[1,72,1024]{2,1,0:T(8,128)} %param.15) | copy-start | bytes 884740
  82.2 40.7 %copy-start.7 = (f32[8,72,128]{2,1,0:T(8,128)S(1)}, f32[8,72,128]{2,1,0:T(8,128)}, u32[]{:S(2)}) copy-start(f32[8,72,128]{2,1,0:T(8,128)} %copy-done.6) | copy-start | bytes 884740
  82.2 40.7 %copy-start.14 = (f32[72,128]{1,0:T(8,128)S(1)}, f32[72,128]{1,0:T(8,128)}, u32[]{:S(2)}) copy-start(f32[72,128]{1,0:T(8,128)} %copy-done.13) | copy-start | bytes 110596
  82.2 40.7 %all-to-all-start.2 = ((bf16[4,128,1024]{2,1,0:T(8,128)(2,1)}), bf16[4,128,1024]{2,1,0:T(8,128)(2,1)S(1)}, u32[]{:S(2)}, u32[]{:S(2)}) async-start(bf16[4,128,1024]{2,1,0:T(8,128)(2,1)} %get-tuple-element.37), calls=%async_computation.2 | async-start | bytes 2097152 | tf_op jit(solution)/shard_map/all_to_all | solution.py:304
  87.2 35.7 %collective-permute-start.2 = (bf16[72,1152]{1,0:T(8,128)(2,1)S(1)}, bf16[72,1152]{1,0:T(8,128)(2,1)S(1)}, u32[]{:S(2)}, u32[]{:S(2)}) collective-permute-start(bf16[72,1152]{1,0:T(8,128)(2,1)S(1)} %copy-done.18), channel_id=1, source_target_pairs={{0,16},{16,0},{1,17},{17,1},{2,18},{18,2},{3,19},{19,3},{4,20},{20... | collective-permute-start | bytes 497672 | tf_op jit(solution)/shard_map/ppermute | solution.py:228
  99.4 14.9 %collective-permute-start.7 = (bf16[8,72,128]{2,1,0:T(8,128)(2,1)S(1)}, bf16[8,72,128]{2,1,0:T(8,128)(2,1)S(1)}, u32[]{:S(2)}, u32[]{:S(2)}) collective-permute-start(bf16[8,72,128]{2,1,0:T(8,128)(2,1)S(1)} %get-tuple-element.34.step), channel_id=1, source_target_pairs={{0,64},{64,0},{128,192},{192,128},{256,320},{320,256},{384,448},{4... | collective-permute-start | bytes 442376 | tf_op jit(solution)/shard_map/ppermute | solution.py:240
  101.3 15.5 %collective-permute-start.8 = (bf16[8,72,128]{2,1,0:T(8,128)(2,1)S(1)}, bf16[8,72,128]{2,1,0:T(8,128)(2,1)S(1)}, u32[]{:S(2)}, u32[]{:S(2)}) collective-permute-start(bf16[8,72,128]{2,1,0:T(8,128)(2,1)S(1)} %get-tuple-element.34.step), channel_id=1, source_target_pairs={{0,128},{64,192},{128,0},{192,64},{256,384},{320,448},{384,256},{4... | collective-permute-start | bytes 442376 | tf_op jit(solution)/shard_map/ppermute | solution.py:240
  103.3 19.6 %collective-permute-start.9 = (bf16[8,72,128]{2,1,0:T(8,128)(2,1)S(1)}, bf16[8,72,128]{2,1,0:T(8,128)(2,1)S(1)}, u32[]{:S(2)}, u32[]{:S(2)}) collective-permute-start(bf16[8,72,128]{2,1,0:T(8,128)(2,1)S(1)} %get-tuple-element.34.step), channel_id=1, source_target_pairs={{0,192},{64,128},{128,64},{192,0},{256,448},{320,384},{384,320},{4... | collective-permute-start | bytes 442376 | tf_op jit(solution)/shard_map/ppermute | solution.py:240
  122.9 0.8 copy-start.16
  123.7 15.2 %copy-start.12 = (f32[1,2304]{1,0:T(1,128)S(1)}, f32[1,2304]{1,0:T(1,128)}, u32[]{:S(2)}) copy-start(f32[1,2304]{1,0:T(1,128)} %gain.1) | copy-start | bytes 27652
  125.8 13.0 %all-to-all-start.3 = ((f32[16,8,128]{2,1,0:T(8,128)}), f32[16,8,128]{2,1,0:T(8,128)S(1)}, u32[]{:S(2)}, u32[]{:S(2)}) async-start(f32[16,8,128]{2,1,0:T(8,128)} %copy-done.10), calls=%async_computation.3 | async-start | bytes 131072 | tf_op jit(solution)/shard_map/all_to_all | solution.py:336
  131.1 9.2 %collective-permute-start.10 = (f32[8,72,128]{2,1,0:T(8,128)S(1)}, f32[8,72,128]{2,1,0:T(8,128)S(1)}, u32[]{:S(2)}, u32[]{:S(2)}) collective-permute-start(f32[8,72,128]{2,1,0:T(8,128)S(1)} %get-tuple-element.43.mine), channel_id=1, source_target_pairs={{0,32},{32,0},{1,33},{33,1},{2,34},{34,2},{3,35},{35,3},{4,36},{36... | collective-permute-start | bytes 884744 | tf_op jit(solution)/shard_map/ppermute | solution.py:228
  (3 other events, 1.9 us)

commit v3 on v2

--- a/solution.py
+++ b/solution.py
@@ -97,8 +97,7 @@
         out[y, block.shape[0] :, :] = turned_grads
 
 
-def dw_body(zl_ref, after, got, mine, theirs, moment, out, step, packed):
-    del after
+def dw_body(zl_ref, got, mine, theirs, moment, out, step, packed):
     part = out.shape[1]
     wide = NX * part
     grads = jnp.concatenate([got[s, wide:, :] for s in range(NY)], axis=1)
@@ -116,9 +115,7 @@
         step[pair] = jnp.where(zl_ref[0] == pair, drift + own, drift).astype(bf16)
 
 
-def dwsum_body(
-    zh_ref, got, weight, own, gain_own, send
-):
+def dwsum_body(zh_ref, got, weight, step, step_got, own, gain_own, send, step_out):
     half = own.shape[0]
     width = own.shape[1]
     low = zh_ref[0] == 0
@@ -140,12 +137,16 @@
     )
     gain_own[...] = packed
     send[:, width:] = packed.astype(bf16)
-
-
-def keys_body(x_ref, done, got, same, before, after, across, step, step_got, out, step_out):
+    step_out[...] = (step[...].astype(f32) + step_got[...].astype(f32)).astype(bf16)
+
+
+def keys_body(
+    x_ref, y_ref, done, got, same, before, after, across, step, step_got, own, up, down, over, step_out
+):
     del done
     part = same.shape[0]
-    for s in range(NY):
+    for to, out in ((0, own), (1, up), (NY - 1, down), (2, over)):
+        s = lax.rem(y_ref[0] + to, NY)
         total = None
         for by, weight in ((0, same), (NX - 1, before), (1, after), (2, across)):
             source = lax.rem(x_ref[0] + by, NX)
@@ -154,33 +155,12 @@
                 rows, weight[...], (((0,), (0,)), ((), ())), preferred_element_type=f32
             )
             total = term if total is None else total + term
-        out[s] = total.astype(bf16)
-    step_out[...] = (step[...].astype(f32) + step_got[...].astype(f32)).astype(bf16)
-
-
-def update_body(
-    zl_ref,
-    own,
-    got,
-    weight,
-    first,
-    second,
-    gain_own,
-    step,
-    step_one,
-    step_two,
-    step_three,
-    outer_mine,
-    packed,
-    keys_got,
-    new_w,
-    new_wf,
-    new_ws,
-    tiles,
-    outer_out,
-    moment_out,
-    keys,
-):
+        out[...] = total.astype(out.dtype)
+    step_out[...] = step[...].astype(f32) + step_got[...].astype(f32)
+
+
+def update_body(after, own, got, weight, first, second, gain_own, new_w, new_wf, new_ws, tiles):
+    del after
     width = own.shape[1]
     grad = own[...] + got[:, :width].astype(f32)
     w, wf, ws = adamw(weight[...].astype(f32), grad, first[...], second[...], rate_weight)
@@ -193,12 +173,13 @@
     total = jnp.transpose(total)[:8]
     for at in range(tiles.shape[0]):
         tiles[at] = total
+
+
+def step_body(zl_ref, step, step_got, outer_mine, packed, outer_out, moment_out):
     half = packed.shape[0]
     mine = jnp.zeros((half, 128), f32)
-    for pair in range(step.shape[0]):
-        both = (step[pair].astype(f32) + step_one[pair].astype(f32)) + (
-            step_two[pair].astype(f32) + step_three[pair].astype(f32)
-        )
+    for pair in range(outer_mine.shape[0]):
+        both = step[pair] + step_got[pair]
         outer_out[pair] = outer_mine[pair] - rate_outer * both
         mine = jnp.where(zl_ref[0] == pair, both, mine)
     moment = packed[...]
@@ -206,10 +187,12 @@
     new = momentum_keep * moment + drift
     moment_out[:half] = new[:, :64]
     moment_out[half:] = new[:, 64:]
-    sums = keys_got[0].astype(f32)
-    for y in range(1, NY):
-        sums = sums + keys_got[y].astype(f32)
-    keys[...] = sums.astype(bf16)
+
+
+def sum_body(own, before, after, across, out):
+    out[...] = (
+        (own[...] + before[...].astype(f32)) + (after[...].astype(f32) + across[...].astype(f32))
+    ).astype(bf16)
 
 
 def join_body(core_ref, mine, got, out):
@@ -269,7 +252,9 @@
         features[0], key_grads[0], norm_gain
     )
     got = lax.all_to_all(sent, "y", 0, 0, tiled=True)
-    pair_weight = call(halves_body, shape((ZH * part, width), bf16), 2, scalars=1)(
+    pair_weight = call(
+        halves_body, shape((ZH * part, width), bf16), 2, scalars=1, flops=int(1.3e10)
+    )(
         zh[None], weight, swap(weight, "zh")
     )
     mine, theirs, outer_mine = call(diff_body, (half, half, half), 2, scalars=1)(
@@ -280,60 +265,46 @@
         (shape((NX, ZH * part, width), bf16), half_short, shape(half.shape[1:], f32)),
         4,
         scalars=1,
+        flops=2 * group * width * tokens * NY,
+    )(zl[None], got, mine, swap(theirs, "core"), outer_momentum)
+    partial = lax.all_to_all(partial, "x", 0, 0, tiled=True)
+    group_weight = ring4(pair_weight, "x")
+
+    own, gain_own, send, step = call(
+        dwsum_body,
+        (
+            shape((part, width), f32),
+            shape((part, 128), f32),
+            shape((part, width + 128), bf16),
+            half_short,
+        ),
+        4,
+        scalars=1,
+    )(zh[None], partial, pair_weight, step, partner(step, 4))
+    keys_sent = shape((tokens, width), bf16)
+    own_keys, up, down, over, step = call(
+        keys_body,
+        (shape((tokens, width), f32), keys_sent, keys_sent, keys_sent, half),
+        7,
+        scalars=2,
         after=1,
         flops=2 * group * width * tokens * NY,
-    )(zl[None], pair_weight, got, mine, swap(theirs, "core"), outer_momentum)
-    partial = lax.all_to_all(partial, "x", 0, 0, tiled=True)
-    group_weight = ring4(pair_weight, "x")
-
-    own, gain_own, send = call(
-        dwsum_body,
-        (shape((part, width), f32), shape((part, 128), f32), shape((part, width + 128), bf16)),
-        2,
-        scalars=1,
-    )(zh[None], partial, pair_weight)
-    grad_got = swap(send, "zh")
-    keys, step = call(
-        keys_body,
-        (shape((NY, tokens, width), bf16), half_short),
-        7,
-        scalars=1,
+    )(x[None], y[None], own, got, *group_weight, step, partner(step, 2))
+
+    moments = shape((part, width), f32)
+    new_w, new_wf, new_ws, tiles = call(
+        update_body,
+        (shape((part, width), bf16), moments, moments, shape((NX * NY, 8, 128), f32)),
+        6,
         after=1,
-        flops=2 * group * width * tokens * NY,
-    )(x[None], own, got, *group_weight, step, partner(step, 4))
-    keys_got = lax.all_to_all(keys, "y", 0, 0, tiled=True)
-
-    moments = shape((part, width), f32)
-    new_w, new_wf, new_ws, tiles, outer_half, new_momentum, keys = call(
-        update_body,
-        (
-            shape((part, width), bf16),
-            moments,
-            moments,
-            shape((NX * NY, 8, 128), f32),
-            half,
-            shape(outer_momentum.shape, f32),
-            shape((tokens, width), bf16),
-        ),
-        13,
-        scalars=1,
-    )(
-        zl[None],
-        own,
-        grad_got,
-        weight,
-        weight_first[0],
-        weight_second[0],
-        gain_own,
-        step,
-        partner(step, 1),
-        partner(step, 2),
-        partner(step, 3),
-        outer_mine,
-        packed,
-        keys_got,
-    )
+    )(own_keys, own, swap(send, "zh"), weight, weight_first[0], weight_second[0], gain_own)
     tiles = lax.all_to_all(tiles, ("x", "y"), 0, 0, tiled=True)
+    keys = call(sum_body, keys_sent, 4)(
+        own_keys, shift(up, "y", 1), shift(down, "y", -1), shift(over, "y", 2)
+    )
+    outer_half, new_momentum = call(
+        step_body, (half, shape(outer_momentum.shape, f32)), 4, scalars=1
+    )(zl[None], step, partner(step, 1), outer_mine, packed)
     new_outer = call(join_body, shape(outer_params.shape, f32), 2, scalars=1)(
         core[None], outer_half, swap(outer_half, "core")
     )

time: 142 us -> 125 us (0.88)
  the two profiles are of different devices: /device:TPU:32 before, /device:TPU:34 now
where the time goes in v3:
time: 125 us; the launch traced here: 124 us
  starting transfers between devices  84.6 us (68%)
  waiting for transfers between devices  17.8 us (14%)
  Pallas kernels  11.2 us (9%)
  local copies, waits for them, and re-layouts  9.16 us (7%)
    ppermute x4, starting transfers between devices, swap(): return lax.ppermute(value, axis, [(0, 1), (1, 0)])  28.5 us
    ppermute x6, starting transfers between devices, shift(): lax.ppermute(value, axis, [(i, (i + by) % size) for i in range(size)])  20.5 us
    ppermute x3, starting transfers between devices, partner(): return lax.ppermute(value, 'zl', [(i, i ^ by) for i in range(ZL)])  15.9 us
    all_to_all x1, starting transfers between devices, local(): tiles = lax.all_to_all(tiles, ('x', 'y'), 0, 0, tiled=True)  10.2 us
    ppermute x4, waiting for transfers between devices, swap(): return lax.ppermute(value, axis, [(0, 1), (1, 0)])  9.96 us
    unnamed x56, local copies, waits for them, and re-layouts  9.06 us
    all_to_all x1, starting transfers between devices, local(): partial = lax.all_to_all(partial, 'x', 0, 0, tiled=True)  4.82 us
    all_to_all x1, starting transfers between devices, local(): got = lax.all_to_all(sent, 'y', 0, 0, tiled=True)  4.61 us
  transfers between devices with their start and end apart: 16, of which 6 were waited for; matrix products, arithmetic and copies ran while one was open for 1% of the time, Pallas kernels for 7%

profile of v3, /device:TPU:34, one launch (start us, length us, event | category | flops | bytes accessed | tf_op | source)
XLA Modules:
  0.0 124.4 jit_solution(5060834459900990642)
XLA Ops:
  0.7 1.1 copy-done.2
  1.7 0.9 copy-done.8
  3.4 1.7 %shard_map.178 = bf16[4,1600,128]{2,1,0:T(8,128)(2,1)} custom-call(bf16[128,2304]{1,0:T(8,128)(2,1)S(1)} %bitcast.17, bf16[128,1024]{1,0:T(8,128)(2,1)S(1)} %bitcast.21, f32[1,2304]{1,0:T(1,128)S(1)} %copy-done.15), custom_call_target="tpu_custom_call" | custom-call | bytes 1048576 | tf_op jit(solution)/shard_map/pallas_call | solution.py:251
  5.1 4.6 %all-to-all-start = ((bf16[4,1600,128]{2,1,0:T(8,128)(2,1)}), bf16[4,1600,128]{2,1,0:T(8,128)(2,1)S(1)}, u32[]{:S(2)}, u32[]{:S(2)}) async-start(bf16[4,1600,128]{2,1,0:T(8,128)(2,1)} %shard_map.178), calls=%async_computation | async-start | bytes 3276800 | tf_op jit(solution)/shard_map/all_to_all | solution.py:254
  10.8 1.9 %collective-permute-start = (f32[8,72,128]{2,1,0:T(8,128)S(1)}, f32[8,72,128]{2,1,0:T(8,128)S(1)}, u32[]{:S(2)}, u32[]{:S(2)}) collective-permute-start(f32[8,72,128]{2,1,0:T(8,128)S(1)} %get-tuple-element.31), channel_id=1, source_target_pairs={{0,32},{32,0},{1,33},{33,1},{2,34},{34,2},{3,35},{35,3},{4,36},{36... | collective-permute-start | bytes 884744 | tf_op jit(solution)/shard_map/ppermute | solution.py:211
  12.7 14.8 %collective-permute-start.1 = (bf16[72,1024]{1,0:T(8,128)(2,1)S(1)}, bf16[72,1024]{1,0:T(8,128)(2,1)S(1)}, u32[]{:S(2)}, u32[]{:S(2)}) collective-permute-start(bf16[72,1024]{1,0:T(8,128)(2,1)S(1)} %bitcast.22), channel_id=1, source_target_pairs={{0,16},{16,0},{1,17},{17,1},{2,18},{18,2},{3,19},{19,3},{4,20},{20... | collective-permute-start | bytes 442376 | tf_op jit(solution)/shard_map/ppermute | solution.py:211
  27.7 3.4 %all-to-all-done.got = bf16[4,1600,128]{2,1,0:T(8,128)(2,1)S(1)} async-done(((bf16[4,1600,128]{2,1,0:T(8,128)(2,1)}), bf16[4,1600,128]{2,1,0:T(8,128)(2,1)S(1)}, u32[]{:S(2)}, u32[]{:S(2)}) %all-to-all-start) | async-done | bytes 1638432 | tf_op jit(solution)/shard_map/all_to_all | solution.py:254
  31.1 1.5 %shard_map.180 = (bf16[4,144,1024]{2,1,0:T(8,128)(2,1)S(1)}, bf16[8,72,128]{2,1,0:T(8,128)(2,1)S(1)}, f32[72,128]{1,0:T(8,128)S(1)}) custom-call(s32[1]{0:T(128)} %bitcast.3.zl_ref, bf16[4,1600,128]{2,1,0:T(8,128)(2,1)S(1)} %all-to-all-done.got, f32[8,72,128]{2,1,0:T(8,128)S(1)} %get-tuple-element.30.mine, f32[8,72,128]{2,1,0:T(8,128)S(1)} %collective-permute-done.theirs, ...), custom_call_target="tpu_custom_call" | custom-call | flops 603979776 | bytes 1048576 | tf_op jit(solution)/shard_map/pallas_call | solution.py:263
  32.6 1.1 copy-done
  34.3 4.8 %all-to-all-start.1 = ((bf16[4,144,1024]{2,1,0:T(8,128)(2,1)}), bf16[4,144,1024]{2,1,0:T(8,128)(2,1)S(1)}, u32[]{:S(2)}, u32[]{:S(2)}) async-start(bf16[4,144,1024]{2,1,0:T(8,128)(2,1)} %copy-done), calls=%async_computation.1 | async-start | bytes 2359296 | tf_op jit(solution)/shard_map/all_to_all | solution.py:270
  39.1 2.3 %collective-permute-done.1.weight_got = bf16[72,1024]{1,0:T(8,128)(2,1)S(1)} collective-permute-done((bf16[72,1024]{1,0:T(8,128)(2,1)S(1)}, bf16[72,1024]{1,0:T(8,128)(2,1)S(1)}, u32[]{:S(2)}, u32[]{:S(2)}) %collective-permute-start.1) | collective-permute-done | bytes 147488 | tf_op jit(solution)/shard_map/ppermute | solution.py:211
  41.5 6.8 %collective-permute-start.2 = (bf16[8,72,128]{2,1,0:T(8,128)(2,1)S(1)}, bf16[8,72,128]{2,1,0:T(8,128)(2,1)S(1)}, u32[]{:S(2)}, u32[]{:S(2)}) collective-permute-start(bf16[8,72,128]{2,1,0:T(8,128)(2,1)S(1)} %get-tuple-element.33.step), channel_id=1, source_target_pairs={{0,256},{64,320},{128,384},{192,448},{256,0},{320,64},{384,128},{4... | collective-permute-start | bytes 442376 | tf_op jit(solution)/shard_map/ppermute | solution.py:223
  48.3 3.4 %collective-permute-start.3 = (bf16[144,1024]{1,0:T(8,128)(2,1)S(1)}, bf16[144,1024]{1,0:T(8,128)(2,1)}, u32[]{:S(2)}, u32[]{:S(2)}) collective-permute-start(bf16[144,1024]{1,0:T(8,128)(2,1)S(1)} %shard_map.181.weight.same), channel_id=1, source_target_pairs={{0,4},{4,8},{8,12},{12,0},{1,5},{5,9},{9,13},{13,1},{2,6},{6,10},{... | collective-permute-start | bytes 884744 | tf_op jit(solution)/shard_map/ppermute | solution.py:215
  51.7 2.5 %collective-permute-start.4 = (bf16[144,1024]{1,0:T(8,128)(2,1)S(1)}, bf16[144,1024]{1,0:T(8,128)(2,1)}, u32[]{:S(2)}, u32[]{:S(2)}) collective-permute-start(bf16[144,1024]{1,0:T(8,128)(2,1)S(1)} %shard_map.181.weight.same), channel_id=1, source_target_pairs={{0,12},{4,0},{8,4},{12,8},{1,13},{5,1},{9,5},{13,9},{2,14},{6,2},{... | collective-permute-start | bytes 884744 | tf_op jit(solution)/shard_map/ppermute | solution.py:215
  54.2 4.0 %collective-permute-start.5 = (bf16[144,1024]{1,0:T(8,128)(2,1)S(1)}, bf16[144,1024]{1,0:T(8,128)(2,1)}, u32[]{:S(2)}, u32[]{:S(2)}) collective-permute-start(bf16[144,1024]{1,0:T(8,128)(2,1)S(1)} %shard_map.181.weight.same), channel_id=1, source_target_pairs={{0,8},{4,12},{8,0},{12,4},{1,9},{5,13},{9,1},{13,5},{2,10},{6,14},... | collective-permute-start | bytes 884744 | tf_op jit(solution)/shard_map/ppermute | solution.py:215
  58.1 1.0 collective-permute-done.2.step_got
  59.8 0.9 copy-done.12
  60.7 0.9 copy-done.14
  61.6 1.0 shard_map.182
  63.2 4.2 %collective-permute-start.6 = (bf16[8,72,128]{2,1,0:T(8,128)(2,1)S(1)}, bf16[8,72,128]{2,1,0:T(8,128)(2,1)S(1)}, u32[]{:S(2)}, u32[]{:S(2)}) collective-permute-start(bf16[8,72,128]{2,1,0:T(8,128)(2,1)S(1)} %get-tuple-element.35.step), channel_id=1, source_target_pairs={{0,128},{64,192},{128,0},{192,64},{256,384},{320,448},{384,256},{4... | collective-permute-start | bytes 442376 | tf_op jit(solution)/shard_map/ppermute | solution.py:223
  67.4 9.9 %collective-permute-start.10 = (bf16[72,1152]{1,0:T(8,128)(2,1)}, bf16[72,1152]{1,0:T(8,128)(2,1)}, u32[]{:S(2)}, u32[]{:S(2)}) collective-permute-start(bf16[72,1152]{1,0:T(8,128)(2,1)} %get-tuple-element.40), channel_id=1, source_target_pairs={{0,16},{16,0},{1,17},{17,1},{2,18},{18,2},{3,19},{19,3},{4,20},{20... | collective-permute-start | bytes 497672 | tf_op jit(solution)/shard_map/ppermute | solution.py:211
  77.4 2.5 %shard_map.183 = (f32[128,1024]{1,0:T(8,128)S(1)}, bf16[128,1024]{1,0:T(8,128)(2,1)S(1)}, bf16[128,1024]{1,0:T(8,128)(2,1)S(1)}, bf16[128,1024]{1,0:T(8,128)(2,1)S(1)}, f32[8,72,128]{2,1,0:T(8,128)S(1)}) custom-call(s32[1]{0:T(128)} %bitcast.x_ref, s32[1]{0:T(128)} %bitcast.1.y_ref, f32[72,1024]{1,0:T(8,128)S(1)} %get-tuple-element.34.done.own, ...), custom_call_target="tpu_custom_call" | custom-call | flops 603979776 | bytes 1048576 | tf_op jit(solution)/shard_map/pallas_call | solution.py:285
  80.0 4.9 %collective-permute-start.11 = (f32[8,72,128]{2,1,0:T(8,128)S(1)}, f32[8,72,128]{2,1,0:T(8,128)S(1)}, u32[]{:S(2)}, u32[]{:S(2)}) collective-permute-start(f32[8,72,128]{2,1,0:T(8,128)S(1)} %get-tuple-element.46.step), channel_id=1, source_target_pairs={{0,64},{64,0},{128,192},{192,128},{256,320},{320,256},{384,448},{4... | collective-permute-start | bytes 884744 | tf_op jit(solution)/shard_map/ppermute | solution.py:223
  84.9 7.6 %collective-permute-done.10.got = bf16[72,1152]{1,0:T(8,128)(2,1)} collective-permute-done((bf16[72,1152]{1,0:T(8,128)(2,1)}, bf16[72,1152]{1,0:T(8,128)(2,1)}, u32[]{:S(2)}, u32[]{:S(2)}) %collective-permute-start.10) | collective-permute-done | bytes 165920 | tf_op jit(solution)/shard_map/ppermute | solution.py:211
  92.6 2.0 %shard_map.185 = (bf16[72,1024]{1,0:T(8,128)(2,1)}, f32[72,1024]{1,0:T(8,128)}, f32[72,1024]{1,0:T(8,128)}, f32[16,8,128]{2,1,0:T(8,128)}) custom-call(f32[128,1024]{1,0:T(8,128)S(1)} %get-tuple-element.36.own.after, f32[72,1024]{1,0:T(8,128)S(1)} %get-tuple-element.34.done.own, bf16[72,1152]{1,0:T(8,128)(2,1)} %collective-permute-done.10.got, ...), custom_call_target="tpu_custom_call" | custom-call | bytes 1048576 | tf_op jit(solution)/shard_map/pallas_call | solution.py:295
  94.6 10.2 %all-to-all-start.2 = ((f32[16,8,128]{2,1,0:T(8,128)}), f32[16,8,128]{2,1,0:T(8,128)S(1)}, u32[]{:S(2)}, u32[]{:S(2)}) async-start(f32[16,8,128]{2,1,0:T(8,128)} %get-tuple-element.45), calls=%async_computation.2 | async-start | bytes 131072 | tf_op jit(solution)/shard_map/all_to_all | solution.py:301
  104.8 3.4 %collective-permute-start.7 = (bf16[128,1024]{1,0:T(8,128)(2,1)}, bf16[128,1024]{1,0:T(8,128)(2,1)S(1)}, u32[]{:S(2)}, u32[]{:S(2)}) collective-permute-start(bf16[128,1024]{1,0:T(8,128)(2,1)} %copy-done.23), channel_id=1, source_target_pairs={{0,1},{1,2},{2,3},{3,0},{4,5},{5,6},{6,7},{7,4},{8,9},{9,10},{10,1... | collective-permute-start | bytes 786440 | tf_op jit(solution)/shard_map/ppermute | solution.py:215
  108.2 3.7 %collective-permute-start.8 = (bf16[128,1024]{1,0:T(8,128)(2,1)}, bf16[128,1024]{1,0:T(8,128)(2,1)S(1)}, u32[]{:S(2)}, u32[]{:S(2)}) collective-permute-start(bf16[128,1024]{1,0:T(8,128)(2,1)} %copy-done.22), channel_id=1, source_target_pairs={{0,3},{1,0},{2,1},{3,2},{4,7},{5,4},{6,5},{7,6},{8,11},{9,8},{10,9... | collective-permute-start | bytes 786440 | tf_op jit(solution)/shard_map/ppermute | solution.py:215
  111.8 3.7 %collective-permute-start.9 = (bf16[128,1024]{1,0:T(8,128)(2,1)}, bf16[128,1024]{1,0:T(8,128)(2,1)S(1)}, u32[]{:S(2)}, u32[]{:S(2)}) collective-permute-start(bf16[128,1024]{1,0:T(8,128)(2,1)} %copy-done.21), channel_id=1, source_target_pairs={{0,2},{1,3},{2,0},{3,1},{4,6},{5,7},{6,4},{7,5},{8,10},{9,11},{10,... | collective-permute-start | bytes 786440 | tf_op jit(solution)/shard_map/ppermute | solution.py:215
  115.8 1.9 %collective-permute-start.12 = (f32[8,72,128]{2,1,0:T(8,128)S(1)}, f32[8,72,128]{2,1,0:T(8,128)S(1)}, u32[]{:S(2)}, u32[]{:S(2)}) collective-permute-start(f32[8,72,128]{2,1,0:T(8,128)S(1)} %get-tuple-element.49.mine), channel_id=1, source_target_pairs={{0,32},{32,0},{1,33},{33,1},{2,34},{34,2},{3,35},{35,3},{4,36},{36... | collective-permute-start | bytes 884744 | tf_op jit(solution)/shard_map/ppermute | solution.py:211
  118.5 3.3 %collective-permute-done.9.across = bf16[128,1024]{1,0:T(8,128)(2,1)S(1)} collective-permute-done((bf16[128,1024]{1,0:T(8,128)(2,1)}, bf16[128,1024]{1,0:T(8,128)(2,1)S(1)}, u32[]{:S(2)}, u32[]{:S(2)}) %collective-permute-start.9) | collective-permute-done | bytes 262176 | tf_op jit(solution)/shard_map/ppermute | solution.py:215
  123.4 1.0 shard_map.187
  (70 shorter events, 6.5 us)
Async XLA Ops:
  5.1 4.6 %copy-start.3 = (bf16[1,144,1024]{2,1,0:T(8,128)(2,1)S(1)}, bf16[1,144,1024]{2,1,0:T(8,128)(2,1)}, u32[]{:S(2)}) copy-start(bf16[1,144,1024]{2,1,0:T(8,128)(2,1)} %param.20) | copy-start | bytes 884740
  5.1 7.6 %copy-start.9 = (bf16[1,72,1024]{2,1,0:T(8,128)(2,1)S(1)}, bf16[1,72,1024]{2,1,0:T(8,128)(2,1)}, u32[]{:S(2)}) copy-start(bf16[1,72,1024]{2,1,0:T(8,128)(2,1)} %param.13) | copy-start | bytes 442372
  5.1 22.5 %copy-start.24 = (f32[144,64]{0,1:T(8,128)S(1)}, f32[144,64]{0,1:T(8,128)}, u32[]{:S(2)}) copy-start(f32[144,64]{0,1:T(8,128)} %param.21) | copy-start | bytes 110596
  5.1 26.0 %all-to-all-start = ((bf16[4,1600,128]{2,1,0:T(8,128)(2,1)}), bf16[4,1600,128]{2,1,0:T(8,128)(2,1)S(1)}, u32[]{:S(2)}, u32[]{:S(2)}) async-start(bf16[4,1600,128]{2,1,0:T(8,128)(2,1)} %shard_map.178), calls=%async_computation | async-start | bytes 3276800 | tf_op jit(solution)/shard_map/all_to_all | solution.py:254
  10.8 16.9 %collective-permute-start = (f32[8,72,128]{2,1,0:T(8,128)S(1)}, f32[8,72,128]{2,1,0:T(8,128)S(1)}, u32[]{:S(2)}, u32[]{:S(2)}) collective-permute-start(f32[8,72,128]{2,1,0:T(8,128)S(1)} %get-tuple-element.31), channel_id=1, source_target_pairs={{0,32},{32,0},{1,33},{33,1},{2,34},{34,2},{3,35},{35,3},{4,36},{36... | collective-permute-start | bytes 884744 | tf_op jit(solution)/shard_map/ppermute | solution.py:211
  12.7 28.7 %collective-permute-start.1 = (bf16[72,1024]{1,0:T(8,128)(2,1)S(1)}, bf16[72,1024]{1,0:T(8,128)(2,1)S(1)}, u32[]{:S(2)}, u32[]{:S(2)}) collective-permute-start(bf16[72,1024]{1,0:T(8,128)(2,1)S(1)} %bitcast.22), channel_id=1, source_target_pairs={{0,16},{16,0},{1,17},{17,1},{2,18},{18,2},{3,19},{19,3},{4,20},{20... | collective-permute-start | bytes 442376 | tf_op jit(solution)/shard_map/ppermute | solution.py:211
  34.3 7.2 %copy-start.11 = (bf16[8,72,128]{2,1,0:T(8,128)(2,1)}, bf16[8,72,128]{2,1,0:T(8,128)(2,1)S(1)}, u32[]{:S(2)}) copy-start(bf16[8,72,128]{2,1,0:T(8,128)(2,1)S(1)} %get-tuple-element.33.step) | copy-start | bytes 442372
  34.3 25.5 %all-to-all-start.1 = ((bf16[4,144,1024]{2,1,0:T(8,128)(2,1)}), bf16[4,144,1024]{2,1,0:T(8,128)(2,1)S(1)}, u32[]{:S(2)}, u32[]{:S(2)}) async-start(bf16[4,144,1024]{2,1,0:T(8,128)(2,1)} %copy-done), calls=%async_computation.1 | async-start | bytes 2359296 | tf_op jit(solution)/shard_map/all_to_all | solution.py:270
  41.5 17.6 %collective-permute-start.2 = (bf16[8,72,128]{2,1,0:T(8,128)(2,1)S(1)}, bf16[8,72,128]{2,1,0:T(8,128)(2,1)S(1)}, u32[]{:S(2)}, u32[]{:S(2)}) collective-permute-start(bf16[8,72,128]{2,1,0:T(8,128)(2,1)S(1)} %get-tuple-element.33.step), channel_id=1, source_target_pairs={{0,256},{64,320},{128,384},{192,448},{256,0},{320,64},{384,128},{4... | collective-permute-start | bytes 442376 | tf_op jit(solution)/shard_map/ppermute | solution.py:223
  48.3 29.0 %collective-permute-start.3 = (bf16[144,1024]{1,0:T(8,128)(2,1)S(1)}, bf16[144,1024]{1,0:T(8,128)(2,1)}, u32[]{:S(2)}, u32[]{:S(2)}) collective-permute-start(bf16[144,1024]{1,0:T(8,128)(2,1)S(1)} %shard_map.181.weight.same), channel_id=1, source_target_pairs={{0,4},{4,8},{8,12},{12,0},{1,5},{5,9},{9,13},{13,1},{2,6},{6,10},{... | collective-permute-start | bytes 884744 | tf_op jit(solution)/shard_map/ppermute | solution.py:215
  51.7 25.6 %collective-permute-start.4 = (bf16[144,1024]{1,0:T(8,128)(2,1)S(1)}, bf16[144,1024]{1,0:T(8,128)(2,1)}, u32[]{:S(2)}, u32[]{:S(2)}) collective-permute-start(bf16[144,1024]{1,0:T(8,128)(2,1)S(1)} %shard_map.181.weight.same), channel_id=1, source_target_pairs={{0,12},{4,0},{8,4},{12,8},{1,13},{5,1},{9,5},{13,9},{2,14},{6,2},{... | collective-permute-start | bytes 884744 | tf_op jit(solution)/shard_map/ppermute | solution.py:215
  54.2 23.2 %collective-permute-start.5 = (bf16[144,1024]{1,0:T(8,128)(2,1)S(1)}, bf16[144,1024]{1,0:T(8,128)(2,1)}, u32[]{:S(2)}, u32[]{:S(2)}) collective-permute-start(bf16[144,1024]{1,0:T(8,128)(2,1)S(1)} %shard_map.181.weight.same), channel_id=1, source_target_pairs={{0,8},{4,12},{8,0},{12,4},{1,9},{5,13},{9,1},{13,5},{2,10},{6,14},... | collective-permute-start | bytes 884744 | tf_op jit(solution)/shard_map/ppermute | solution.py:215
  63.2 14.1 %collective-permute-start.6 = (bf16[8,72,128]{2,1,0:T(8,128)(2,1)S(1)}, bf16[8,72,128]{2,1,0:T(8,128)(2,1)S(1)}, u32[]{:S(2)}, u32[]{:S(2)}) collective-permute-start(bf16[8,72,128]{2,1,0:T(8,128)(2,1)S(1)} %get-tuple-element.35.step), channel_id=1, source_target_pairs={{0,128},{64,192},{128,0},{192,64},{256,384},{320,448},{384,256},{4... | collective-permute-start | bytes 442376 | tf_op jit(solution)/shard_map/ppermute | solution.py:223
  67.4 25.1 %collective-permute-start.10 = (bf16[72,1152]{1,0:T(8,128)(2,1)}, bf16[72,1152]{1,0:T(8,128)(2,1)}, u32[]{:S(2)}, u32[]{:S(2)}) collective-permute-start(bf16[72,1152]{1,0:T(8,128)(2,1)} %get-tuple-element.40), channel_id=1, source_target_pairs={{0,16},{16,0},{1,17},{17,1},{2,18},{18,2},{3,19},{19,3},{4,20},{20... | collective-permute-start | bytes 497672 | tf_op jit(solution)/shard_map/ppermute | solution.py:211
  77.3 15.2 %copy-start.6 = (f32[1,72,1024]{2,1,0:T(8,128)S(1)}, f32[1,72,1024]{2,1,0:T(8,128)}, u32[]{:S(2)}) copy-start(f32[1,72,1024]{2,1,0:T(8,128)} %param.14) | copy-start | bytes 884740
  77.3 15.2 %copy-start.7 = (f32[1,72,1024]{2,1,0:T(8,128)S(1)}, f32[1,72,1024]{2,1,0:T(8,128)}, u32[]{:S(2)}) copy-start(f32[1,72,1024]{2,1,0:T(8,128)} %param.15) | copy-start | bytes 884740
  77.4 15.2 %copy-start.10 = (bf16[1,72,1024]{2,1,0:T(8,128)(2,1)S(1)}, bf16[1,72,1024]{2,1,0:T(8,128)(2,1)}, u32[]{:S(2)}) copy-start(bf16[1,72,1024]{2,1,0:T(8,128)(2,1)} %param.13) | copy-start | bytes 442372
  77.4 15.2 %copy-start.20 = (f32[72,128]{1,0:T(8,128)S(1)}, f32[72,128]{1,0:T(8,128)}, u32[]{:S(2)}) copy-start(f32[72,128]{1,0:T(8,128)} %copy-done.19) | copy-start | bytes 110596
  79.9 14.7 %copy-start.21 = (bf16[128,1024]{1,0:T(8,128)(2,1)}, bf16[128,1024]{1,0:T(8,128)(2,1)S(1)}, u32[]{:S(2)}) copy-start(bf16[128,1024]{1,0:T(8,128)(2,1)S(1)} %get-tuple-element.39) | copy-start | bytes 786436
  79.9 14.7 %copy-start.22 = (bf16[128,1024]{1,0:T(8,128)(2,1)}, bf16[128,1024]{1,0:T(8,128)(2,1)S(1)}, u32[]{:S(2)}) copy-start(bf16[128,1024]{1,0:T(8,128)(2,1)S(1)} %get-tuple-element.38) | copy-start | bytes 786436
  79.9 14.7 %copy-start.23 = (bf16[128,1024]{1,0:T(8,128)(2,1)}, bf16[128,1024]{1,0:T(8,128)(2,1)S(1)}, u32[]{:S(2)}) copy-start(bf16[128,1024]{1,0:T(8,128)(2,1)S(1)} %get-tuple-element.37) | copy-start | bytes 786436
  79.9 35.7 %copy-start.5 = (f32[8,72,128]{2,1,0:T(8,128)S(1)}, f32[8,72,128]{2,1,0:T(8,128)}, u32[]{:S(2)}) copy-start(f32[8,72,128]{2,1,0:T(8,128)} %copy-done.4) | copy-start | bytes 884740
  80.0 35.7 %copy-start.18 = (f32[72,128]{1,0:T(8,128)S(1)}, f32[72,128]{1,0:T(8,128)}, u32[]{:S(2)}) copy-start(f32[72,128]{1,0:T(8,128)} %copy-done.17) | copy-start | bytes 110596
  80.0 37.8 %copy-start.16 = (f32[1,2304]{1,0:T(1,128)S(1)}, f32[1,2304]{1,0:T(1,128)}, u32[]{:S(2)}) copy-start(f32[1,2304]{1,0:T(1,128)} %gain.1) | copy-start | bytes 27652
  80.0 37.8 %copy-start.25 = (f32[1,2304]{1,0:T(1,128)S(1)}, f32[1,2304]{1,0:T(1,128)}, u32[]{:S(2)}) copy-start(f32[1,2304]{1,0:T(1,128)} %param.18) | copy-start | bytes 27652
  80.0 37.8 %copy-start.26 = (f32[1,2304]{1,0:T(1,128)S(1)}, f32[1,2304]{1,0:T(1,128)}, u32[]{:S(2)}) copy-start(f32[1,2304]{1,0:T(1,128)} %param.17) | copy-start | bytes 27652
  80.0 35.7 %collective-permute-start.11 = (f32[8,72,128]{2,1,0:T(8,128)S(1)}, f32[8,72,128]{2,1,0:T(8,128)S(1)}, u32[]{:S(2)}, u32[]{:S(2)}) collective-permute-start(f32[8,72,128]{2,1,0:T(8,128)S(1)} %get-tuple-element.46.step), channel_id=1, source_target_pairs={{0,64},{64,0},{128,192},{192,128},{256,320},{320,256},{384,448},{4... | collective-permute-start | bytes 884744 | tf_op jit(solution)/shard_map/ppermute | solution.py:223
  94.6 20.9 %all-to-all-start.2 = ((f32[16,8,128]{2,1,0:T(8,128)}), f32[16,8,128]{2,1,0:T(8,128)S(1)}, u32[]{:S(2)}, u32[]{:S(2)}) async-start(f32[16,8,128]{2,1,0:T(8,128)} %get-tuple-element.45), calls=%async_computation.2 | async-start | bytes 131072 | tf_op jit(solution)/shard_map/all_to_all | solution.py:301
  104.8 13.6 %collective-permute-start.7 = (bf16[128,1024]{1,0:T(8,128)(2,1)}, bf16[128,1024]{1,0:T(8,128)(2,1)S(1)}, u32[]{:S(2)}, u32[]{:S(2)}) collective-permute-start(bf16[128,1024]{1,0:T(8,128)(2,1)} %copy-done.23), channel_id=1, source_target_pairs={{0,1},{1,2},{2,3},{3,0},{4,5},{5,6},{6,7},{7,4},{8,9},{9,10},{10,1... | collective-permute-start | bytes 786440 | tf_op jit(solution)/shard_map/ppermute | solution.py:215
  108.2 10.4 %collective-permute-start.8 = (bf16[128,1024]{1,0:T(8,128)(2,1)}, bf16[128,1024]{1,0:T(8,128)(2,1)S(1)}, u32[]{:S(2)}, u32[]{:S(2)}) collective-permute-start(bf16[128,1024]{1,0:T(8,128)(2,1)} %copy-done.22), channel_id=1, source_target_pairs={{0,3},{1,0},{2,1},{3,2},{4,7},{5,4},{6,5},{7,6},{8,11},{9,8},{10,9... | collective-permute-start | bytes 786440 | tf_op jit(solution)/shard_map/ppermute | solution.py:215
  111.8 10.0 %collective-permute-start.9 = (bf16[128,1024]{1,0:T(8,128)(2,1)}, bf16[128,1024]{1,0:T(8,128)(2,1)S(1)}, u32[]{:S(2)}, u32[]{:S(2)}) collective-permute-start(bf16[128,1024]{1,0:T(8,128)(2,1)} %copy-done.21), channel_id=1, source_target_pairs={{0,2},{1,3},{2,0},{3,1},{4,6},{5,7},{6,4},{7,5},{8,10},{9,11},{10,... | collective-permute-start | bytes 786440 | tf_op jit(solution)/shard_map/ppermute | solution.py:215
  115.8 7.5 %collective-permute-start.12 = (f32[8,72,128]{2,1,0:T(8,128)S(1)}, f32[8,72,128]{2,1,0:T(8,128)S(1)}, u32[]{:S(2)}, u32[]{:S(2)}) collective-permute-start(f32[8,72,128]{2,1,0:T(8,128)S(1)} %get-tuple-element.49.mine), channel_id=1, source_target_pairs={{0,32},{32,0},{1,33},{33,1},{2,34},{34,2},{3,35},{35,3},{4,36},{36... | collective-permute-start | bytes 884744 | tf_op jit(solution)/shard_map/ppermute | solution.py:211
  (11 other events, 12.8 us)

commit v4 on v3

--- a/solution.py
+++ b/solution.py
@@ -28,13 +28,13 @@
 SMEM = pl.BlockSpec(memory_space=pltpu.SMEM)
 
 
-def call(body, out_shape, n_in, *, scalars=0, after=0, flops=0, moved=1 << 20):
+def call(body, out_shape, n_in, *, scalars=0, after=0, flops=0, moved=1 << 20, vmem=40):
     return pl.pallas_call(
         body,
         out_shape=out_shape,
         in_specs=[SMEM] * scalars + [ANY] * after + [VMEM] * n_in,
         out_specs=jax.tree.map(lambda _: VMEM, out_shape),
-        compiler_params=pltpu.CompilerParams(vmem_limit_bytes=40 << 20),
+        compiler_params=pltpu.CompilerParams(vmem_limit_bytes=vmem << 20),
         cost_estimate=pl.CostEstimate(flops=flops, bytes_accessed=moved, transcendentals=0),
     )
 
@@ -248,7 +248,7 @@
     half = shape((width // 128, rows // 2, 128), f32)
     half_short = shape(half.shape, bf16)
 
-    sent = call(norm_body, shape((NY, group + width, tokens), bf16), 3)(
+    sent = call(norm_body, shape((NY, group + width, tokens), bf16), 3, vmem=62)(
         features[0], key_grads[0], norm_gain
     )
     got = lax.all_to_all(sent, "y", 0, 0, tiled=True)
@@ -280,6 +280,7 @@
         ),
         4,
         scalars=1,
+        vmem=62,
     )(zh[None], partial, pair_weight, step, partner(step, 4))
     keys_sent = shape((tokens, width), bf16)
     own_keys, up, down, over, step = call(
@@ -288,8 +289,9 @@
         7,
         scalars=2,
         after=1,
+        vmem=62,
         flops=2 * group * width * tokens * NY,
-    )(x[None], y[None], own, got, *group_weight, step, partner(step, 2))
+    )(x[None], y[None], send, got, *group_weight, step, partner(step, 2))
 
     moments = shape((part, width), f32)
     new_w, new_wf, new_ws, tiles = call(
@@ -297,7 +299,7 @@
         (shape((part, width), bf16), moments, moments, shape((NX * NY, 8, 128), f32)),
         6,
         after=1,
-    )(own_keys, own, swap(send, "zh"), weight, weight_first[0], weight_second[0], gain_own)
+    )(up, own, swap(send, "zh"), weight, weight_first[0], weight_second[0], gain_own)
     tiles = lax.all_to_all(tiles, ("x", "y"), 0, 0, tiled=True)
     keys = call(sum_body, keys_sent, 4)(
         own_keys, shift(up, "y", 1), shift(down, "y", -1), shift(over, "y", 2)

time: 125 us -> 121 us (0.968)
  local copies, waits for them, and re-layouts: 9.16 us -> 3.27 us
  Pallas kernels: 11.2 us -> 15.4 us
  waiting for transfers between devices: 17.8 us -> 13.7 us
  starting transfers between devices: 84.6 us -> 86.2 us
    unnamed x56 -> x42, local copies, waits for them, and re-layouts: 9.06 us -> 3.17 us
    ppermute x4, waiting for transfers between devices: 9.96 us -> 6.27 us  [swap(): return lax.ppermute(value, axis, [(0, 1), (1, 0)])]
    pallas_call x1, Pallas kernels: 0.97 us -> 2.46 us  [local(): call(dwsum_body, (shape((part, width), f32), shape((part, 128), f32), sha...]
    pallas_call x1, Pallas kernels: 2.52 us -> 3.98 us  [local(): call(keys_body, (shape((tokens, width), f32), keys_sent, keys_sent, keys_...]
    all_to_all x1, starting transfers between devices: 10.2 us -> 11.5 us  [local(): tiles = lax.all_to_all(tiles, ('x', 'y'), 0, 0, tiled=True)]
  transfers between devices with their start and end apart: 16 -> 16, of which waited for: 6 -> 5; matrix products, arithmetic and copies ran while one was open for 1% -> 2% of each run, Pallas kernels for 7% -> 10%
where the time goes in v4:
time: 121 us; the launch traced here: 120 us
  starting transfers between devices  86.2 us (71%)
  Pallas kernels  15.4 us (13%)
  waiting for transfers between devices  13.7 us (11%)
  local copies, waits for them, and re-layouts  3.27 us (3%)
    ppermute x4, starting transfers between devices, swap(): return lax.ppermute(value, axis, [(0, 1), (1, 0)])  28.6 us
    ppermute x6, starting transfers between devices, shift(): lax.ppermute(value, axis, [(i, (i + by) % size) for i in range(size)])  20.5 us
    ppermute x3, starting transfers between devices, partner(): return lax.ppermute(value, 'zl', [(i, i ^ by) for i in range(ZL)])  16.1 us
    all_to_all x1, starting transfers between devices, local(): tiles = lax.all_to_all(tiles, ('x', 'y'), 0, 0, tiled=True)  11.5 us
    ppermute x4, waiting for transfers between devices, swap(): return lax.ppermute(value, axis, [(0, 1), (1, 0)])  6.27 us
    all_to_all x1, starting transfers between devices, local(): partial = lax.all_to_all(partial, 'x', 0, 0, tiled=True)  4.82 us
    all_to_all x1, starting transfers between devices, local(): got = lax.all_to_all(sent, 'y', 0, 0, tiled=True)  4.59 us
    pallas_call x1, Pallas kernels, local(): call(keys_body, (shape((tokens, width), f32), keys_sent, keys_sent, keys_...  3.98 us
  transfers between devices with their start and end apart: 16, of which 5 were waited for; matrix products, arithmetic and copies ran while one was open for 2% of the time, Pallas kernels for 10%

profile of v4, /device:TPU:34, one launch (start us, length us, event | category | flops | bytes accessed | tf_op | source)
XLA Modules:
  0.0 120.2 jit_solution(14559999398173751349)
XLA Ops:
  0.6 2.9 %shard_map.178 = bf16[4,1600,128]{2,1,0:T(8,128)(2,1)} custom-call(bf16[128,2304]{1,0:T(8,128)(2,1)} %bitcast.23, bf16[128,1024]{1,0:T(8,128)(2,1)} %bitcast.24, f32[1,2304]{1,0:T(1,128)} %gain.1), custom_call_target="tpu_custom_call" | custom-call | bytes 1048576 | tf_op jit(solution)/shard_map/pallas_call | solution.py:251
  3.5 4.6 %all-to-all-start = ((bf16[4,1600,128]{2,1,0:T(8,128)(2,1)}), bf16[4,1600,128]{2,1,0:T(8,128)(2,1)S(1)}, u32[]{:S(2)}, u32[]{:S(2)}) async-start(bf16[4,1600,128]{2,1,0:T(8,128)(2,1)} %shard_map.178), calls=%async_computation | async-start | bytes 3276800 | tf_op jit(solution)/shard_map/all_to_all | solution.py:254
  8.5 1.9 %collective-permute-start = (f32[8,72,128]{2,1,0:T(8,128)S(1)}, f32[8,72,128]{2,1,0:T(8,128)S(1)}, u32[]{:S(2)}, u32[]{:S(2)}) collective-permute-start(f32[8,72,128]{2,1,0:T(8,128)S(1)} %get-tuple-element.31), channel_id=1, source_target_pairs={{0,32},{32,0},{1,33},{33,1},{2,34},{34,2},{3,35},{35,3},{4,36},{36... | collective-permute-start | bytes 884744 | tf_op jit(solution)/shard_map/ppermute | solution.py:211
  10.4 14.8 %collective-permute-start.1 = (bf16[72,1024]{1,0:T(8,128)(2,1)S(1)}, bf16[72,1024]{1,0:T(8,128)(2,1)S(1)}, u32[]{:S(2)}, u32[]{:S(2)}) collective-permute-start(bf16[72,1024]{1,0:T(8,128)(2,1)S(1)} %bitcast.20), channel_id=1, source_target_pairs={{0,16},{16,0},{1,17},{17,1},{2,18},{18,2},{3,19},{19,3},{4,20},{20... | collective-permute-start | bytes 442376 | tf_op jit(solution)/shard_map/ppermute | solution.py:211
  25.3 0.9 copy.22.moment
  26.2 3.3 %all-to-all-done.got = bf16[4,1600,128]{2,1,0:T(8,128)(2,1)S(1)} async-done(((bf16[4,1600,128]{2,1,0:T(8,128)(2,1)}), bf16[4,1600,128]{2,1,0:T(8,128)(2,1)S(1)}, u32[]{:S(2)}, u32[]{:S(2)}) %all-to-all-start) | async-done | bytes 1638432 | tf_op jit(solution)/shard_map/all_to_all | solution.py:254
  29.5 2.5 %shard_map.180 = (bf16[4,144,1024]{2,1,0:T(8,128)(2,1)}, bf16[8,72,128]{2,1,0:T(8,128)(2,1)S(1)}, f32[72,128]{1,0:T(8,128)S(1)}) custom-call(s32[1]{0:T(128)} %bitcast.3.zl_ref, bf16[4,1600,128]{2,1,0:T(8,128)(2,1)S(1)} %all-to-all-done.got, f32[8,72,128]{2,1,0:T(8,128)S(1)} %get-tuple-element.30.mine, f32[8,72,128]{2,1,0:T(8,128)S(1)} %collective-permute-done.theirs, ...), custom_call_target="tpu_custom_call" | custom-call | flops 603979776 | bytes 1048576 | tf_op jit(solution)/shard_map/pallas_call | solution.py:263
  32.0 4.8 %all-to-all-start.1 = ((bf16[4,144,1024]{2,1,0:T(8,128)(2,1)}), bf16[4,144,1024]{2,1,0:T(8,128)(2,1)}, u32[]{:S(2)}, u32[]{:S(2)}) async-start(bf16[4,144,1024]{2,1,0:T(8,128)(2,1)} %get-tuple-element.32), calls=%async_computation.1 | async-start | bytes 2359296 | tf_op jit(solution)/shard_map/all_to_all | solution.py:270
  36.9 2.3 %collective-permute-done.1.weight_got = bf16[72,1024]{1,0:T(8,128)(2,1)S(1)} collective-permute-done((bf16[72,1024]{1,0:T(8,128)(2,1)S(1)}, bf16[72,1024]{1,0:T(8,128)(2,1)S(1)}, u32[]{:S(2)}, u32[]{:S(2)}) %collective-permute-start.1) | collective-permute-done | bytes 147488 | tf_op jit(solution)/shard_map/ppermute | solution.py:211
  39.2 6.9 %collective-permute-start.2 = (bf16[8,72,128]{2,1,0:T(8,128)(2,1)S(1)}, bf16[8,72,128]{2,1,0:T(8,128)(2,1)S(1)}, u32[]{:S(2)}, u32[]{:S(2)}) collective-permute-start(bf16[8,72,128]{2,1,0:T(8,128)(2,1)S(1)} %get-tuple-element.33.step), channel_id=1, source_target_pairs={{0,256},{64,320},{128,384},{192,448},{256,0},{320,64},{384,128},{4... | collective-permute-start | bytes 442376 | tf_op jit(solution)/shard_map/ppermute | solution.py:223
  46.1 3.4 %collective-permute-start.3 = (bf16[144,1024]{1,0:T(8,128)(2,1)S(1)}, bf16[144,1024]{1,0:T(8,128)(2,1)S(1)}, u32[]{:S(2)}, u32[]{:S(2)}) collective-permute-start(bf16[144,1024]{1,0:T(8,128)(2,1)S(1)} %shard_map.181.weight.same), channel_id=1, source_target_pairs={{0,4},{4,8},{8,12},{12,0},{1,5},{5,9},{9,13},{13,1},{2,6},{6,10},{... | collective-permute-start | bytes 884744 | tf_op jit(solution)/shard_map/ppermute | solution.py:215
  49.5 2.5 %collective-permute-start.4 = (bf16[144,1024]{1,0:T(8,128)(2,1)S(1)}, bf16[144,1024]{1,0:T(8,128)(2,1)S(1)}, u32[]{:S(2)}, u32[]{:S(2)}) collective-permute-start(bf16[144,1024]{1,0:T(8,128)(2,1)S(1)} %shard_map.181.weight.same), channel_id=1, source_target_pairs={{0,12},{4,0},{8,4},{12,8},{1,13},{5,1},{9,5},{13,9},{2,14},{6,2},{... | collective-permute-start | bytes 884744 | tf_op jit(solution)/shard_map/ppermute | solution.py:215
  51.9 4.0 %collective-permute-start.5 = (bf16[144,1024]{1,0:T(8,128)(2,1)S(1)}, bf16[144,1024]{1,0:T(8,128)(2,1)}, u32[]{:S(2)}, u32[]{:S(2)}) collective-permute-start(bf16[144,1024]{1,0:T(8,128)(2,1)S(1)} %shard_map.181.weight.same), channel_id=1, source_target_pairs={{0,8},{4,12},{8,0},{12,4},{1,9},{5,13},{9,1},{13,5},{2,10},{6,14},... | collective-permute-start | bytes 884744 | tf_op jit(solution)/shard_map/ppermute | solution.py:215
  55.9 0.9 collective-permute-done.2.step_got
  57.5 2.5 %shard_map.182 = (f32[72,1024]{1,0:T(8,128)}, f32[72,128]{1,0:T(8,128)}, bf16[72,1152]{1,0:T(8,128)(2,1)}, bf16[8,72,128]{2,1,0:T(8,128)(2,1)}) custom-call(s32[1]{0:T(128)} %bitcast.2.zh_ref, bf16[4,144,1024]{2,1,0:T(8,128)(2,1)} %all-to-all-done.1.got, bf16[144,1024]{1,0:T(8,128)(2,1)} %copy-done.1, bf16[8,72,128]{2,1,0:T(8,128)(2,1)} %copy-done.10, ...), custom_call_target="tpu_custom_call" | custom-call | bytes 1048576 | tf_op jit(solution)/shard_map/pallas_call | solution.py:273
  60.0 4.3 %collective-permute-start.6 = (bf16[8,72,128]{2,1,0:T(8,128)(2,1)}, bf16[8,72,128]{2,1,0:T(8,128)(2,1)S(1)}, u32[]{:S(2)}, u32[]{:S(2)}) collective-permute-start(bf16[8,72,128]{2,1,0:T(8,128)(2,1)} %get-tuple-element.35.step), channel_id=1, source_target_pairs={{0,128},{64,192},{128,0},{192,64},{256,384},{320,448},{384,256},{4... | collective-permute-start | bytes 442376 | tf_op jit(solution)/shard_map/ppermute | solution.py:223
  64.2 10.0 %collective-permute-start.10 = (bf16[72,1152]{1,0:T(8,128)(2,1)}, bf16[72,1152]{1,0:T(8,128)(2,1)S(1)}, u32[]{:S(2)}, u32[]{:S(2)}) collective-permute-start(bf16[72,1152]{1,0:T(8,128)(2,1)} %get-tuple-element.34.done), channel_id=1, source_target_pairs={{0,16},{16,0},{1,17},{17,1},{2,18},{18,2},{3,19},{19,3},{4,20},{20... | collective-permute-start | bytes 497672 | tf_op jit(solution)/shard_map/ppermute | solution.py:211
  74.3 0.7 copy-done.13
  75.1 4.0 %shard_map.183 = (f32[128,1024]{1,0:T(8,128)}, bf16[128,1024]{1,0:T(8,128)(2,1)}, bf16[128,1024]{1,0:T(8,128)(2,1)}, bf16[128,1024]{1,0:T(8,128)(2,1)}, f32[8,72,128]{2,1,0:T(8,128)}) custom-call(s32[1]{0:T(128)} %bitcast.x_ref, s32[1]{0:T(128)} %bitcast.1.y_ref, bf16[72,1152]{1,0:T(8,128)(2,1)} %get-tuple-element.34.done, bf16[4,1600,128]{2,1,0:T(8,128)(2,1)} %copy-done, ...), custom_call_target="tpu_custom_call" | custom-call | flops 603979776 | bytes 1048576 | tf_op jit(solution)/shard_map/pallas_call | solution.py:286
  79.1 5.0 %collective-permute-start.11 = (f32[8,72,128]{2,1,0:T(8,128)}, f32[8,72,128]{2,1,0:T(8,128)S(1)}, u32[]{:S(2)}, u32[]{:S(2)}) collective-permute-start(f32[8,72,128]{2,1,0:T(8,128)} %get-tuple-element.46.step), channel_id=1, source_target_pairs={{0,64},{64,0},{128,192},{192,128},{256,320},{320,256},{384,448},{4... | collective-permute-start | bytes 884744 | tf_op jit(solution)/shard_map/ppermute | solution.py:223
  84.2 4.0 %collective-permute-done.10.got = bf16[72,1152]{1,0:T(8,128)(2,1)S(1)} collective-permute-done((bf16[72,1152]{1,0:T(8,128)(2,1)}, bf16[72,1152]{1,0:T(8,128)(2,1)S(1)}, u32[]{:S(2)}, u32[]{:S(2)}) %collective-permute-start.10) | collective-permute-done | bytes 165920 | tf_op jit(solution)/shard_map/ppermute | solution.py:211
  88.2 1.1 shard_map.185
  89.3 11.5 %all-to-all-start.2 = ((f32[16,8,128]{2,1,0:T(8,128)}), f32[16,8,128]{2,1,0:T(8,128)S(1)}, u32[]{:S(2)}, u32[]{:S(2)}) async-start(f32[16,8,128]{2,1,0:T(8,128)} %get-tuple-element.45), calls=%async_computation.2 | async-start | bytes 131072 | tf_op jit(solution)/shard_map/all_to_all | solution.py:303
  100.8 3.4 %collective-permute-start.7 = (bf16[128,1024]{1,0:T(8,128)(2,1)}, bf16[128,1024]{1,0:T(8,128)(2,1)S(1)}, u32[]{:S(2)}, u32[]{:S(2)}) collective-permute-start(bf16[128,1024]{1,0:T(8,128)(2,1)} %get-tuple-element.37.after), channel_id=1, source_target_pairs={{0,1},{1,2},{2,3},{3,0},{4,5},{5,6},{6,7},{7,4},{8,9},{9,10},{10,1... | collective-permute-start | bytes 786440 | tf_op jit(solution)/shard_map/ppermute | solution.py:215
  104.1 3.7 %collective-permute-start.8 = (bf16[128,1024]{1,0:T(8,128)(2,1)}, bf16[128,1024]{1,0:T(8,128)(2,1)S(1)}, u32[]{:S(2)}, u32[]{:S(2)}) collective-permute-start(bf16[128,1024]{1,0:T(8,128)(2,1)} %get-tuple-element.38), channel_id=1, source_target_pairs={{0,3},{1,0},{2,1},{3,2},{4,7},{5,4},{6,5},{7,6},{8,11},{9,8},{10,9... | collective-permute-start | bytes 786440 | tf_op jit(solution)/shard_map/ppermute | solution.py:215
  107.8 3.7 %collective-permute-start.9 = (bf16[128,1024]{1,0:T(8,128)(2,1)S(1)}, bf16[128,1024]{1,0:T(8,128)(2,1)S(1)}, u32[]{:S(2)}, u32[]{:S(2)}) collective-permute-start(bf16[128,1024]{1,0:T(8,128)(2,1)S(1)} %copy-done.19), channel_id=1, source_target_pairs={{0,2},{1,3},{2,0},{3,1},{4,6},{5,7},{6,4},{7,5},{8,10},{9,11},{10,... | collective-permute-start | bytes 786440 | tf_op jit(solution)/shard_map/ppermute | solution.py:215
  111.8 1.9 %collective-permute-start.12 = (f32[8,72,128]{2,1,0:T(8,128)S(1)}, f32[8,72,128]{2,1,0:T(8,128)S(1)}, u32[]{:S(2)}, u32[]{:S(2)}) collective-permute-start(f32[8,72,128]{2,1,0:T(8,128)S(1)} %get-tuple-element.49.mine), channel_id=1, source_target_pairs={{0,32},{32,0},{1,33},{33,1},{2,34},{34,2},{3,35},{35,3},{4,36},{36... | collective-permute-start | bytes 884744 | tf_op jit(solution)/shard_map/ppermute | solution.py:211
  113.7 0.7 multiply_subtract_fusion
  114.4 3.2 %collective-permute-done.9.across = bf16[128,1024]{1,0:T(8,128)(2,1)S(1)} collective-permute-done((bf16[128,1024]{1,0:T(8,128)(2,1)S(1)}, bf16[128,1024]{1,0:T(8,128)(2,1)S(1)}, u32[]{:S(2)}, u32[]{:S(2)}) %collective-permute-start.9) | collective-permute-done | bytes 262176 | tf_op jit(solution)/shard_map/ppermute | solution.py:215
  117.6 0.8 shard_map.184
  118.4 0.7 copy.24
  119.1 1.0 shard_map.187
  (56 shorter events, 1.5 us)
Async XLA Ops:
  3.5 4.6 %copy-start.2 = (f32[144,1024]{1,0:T(8,128)S(1)}, f32[144,1024]{1,0:T(8,128)}, u32[]{:S(2)}) copy-start(f32[144,1024]{1,0:T(8,128)} %outer.1) | copy-start | bytes 1769476
  3.5 4.6 %copy-start.4 = (bf16[1,144,1024]{2,1,0:T(8,128)(2,1)S(1)}, bf16[1,144,1024]{2,1,0:T(8,128)(2,1)}, u32[]{:S(2)}) copy-start(bf16[1,144,1024]{2,1,0:T(8,128)(2,1)} %param.20) | copy-start | bytes 884740
  3.5 6.9 %copy-start.9 = (bf16[1,72,1024]{2,1,0:T(8,128)(2,1)S(1)}, bf16[1,72,1024]{2,1,0:T(8,128)(2,1)}, u32[]{:S(2)}) copy-start(bf16[1,72,1024]{2,1,0:T(8,128)(2,1)} %param.13) | copy-start | bytes 442372
  3.5 26.0 %all-to-all-start = ((bf16[4,1600,128]{2,1,0:T(8,128)(2,1)}), bf16[4,1600,128]{2,1,0:T(8,128)(2,1)S(1)}, u32[]{:S(2)}, u32[]{:S(2)}) async-start(bf16[4,1600,128]{2,1,0:T(8,128)(2,1)} %shard_map.178), calls=%async_computation | async-start | bytes 3276800 | tf_op jit(solution)/shard_map/all_to_all | solution.py:254
  8.5 17.7 %collective-permute-start = (f32[8,72,128]{2,1,0:T(8,128)S(1)}, f32[8,72,128]{2,1,0:T(8,128)S(1)}, u32[]{:S(2)}, u32[]{:S(2)}) collective-permute-start(f32[8,72,128]{2,1,0:T(8,128)S(1)} %get-tuple-element.31), channel_id=1, source_target_pairs={{0,32},{32,0},{1,33},{33,1},{2,34},{34,2},{3,35},{35,3},{4,36},{36... | collective-permute-start | bytes 884744 | tf_op jit(solution)/shard_map/ppermute | solution.py:211
  10.4 28.7 %collective-permute-start.1 = (bf16[72,1024]{1,0:T(8,128)(2,1)S(1)}, bf16[72,1024]{1,0:T(8,128)(2,1)S(1)}, u32[]{:S(2)}, u32[]{:S(2)}) collective-permute-start(bf16[72,1024]{1,0:T(8,128)(2,1)S(1)} %bitcast.20), channel_id=1, source_target_pairs={{0,16},{16,0},{1,17},{17,1},{2,18},{18,2},{3,19},{19,3},{4,20},{20... | collective-permute-start | bytes 442376 | tf_op jit(solution)/shard_map/ppermute | solution.py:211
  29.5 2.5 %copy-start = (bf16[4,1600,128]{2,1,0:T(8,128)(2,1)}, bf16[4,1600,128]{2,1,0:T(8,128)(2,1)S(1)}, u32[]{:S(2)}) copy-start(bf16[4,1600,128]{2,1,0:T(8,128)(2,1)S(1)} %all-to-all-done.got) | copy-start | bytes 4915204
  32.0 7.2 %copy-start.10 = (bf16[8,72,128]{2,1,0:T(8,128)(2,1)}, bf16[8,72,128]{2,1,0:T(8,128)(2,1)S(1)}, u32[]{:S(2)}) copy-start(bf16[8,72,128]{2,1,0:T(8,128)(2,1)S(1)} %get-tuple-element.33.step) | copy-start | bytes 442372
  32.0 24.8 %all-to-all-start.1 = ((bf16[4,144,1024]{2,1,0:T(8,128)(2,1)}), bf16[4,144,1024]{2,1,0:T(8,128)(2,1)}, u32[]{:S(2)}, u32[]{:S(2)}) async-start(bf16[4,144,1024]{2,1,0:T(8,128)(2,1)} %get-tuple-element.32), calls=%async_computation.1 | async-start | bytes 2359296 | tf_op jit(solution)/shard_map/all_to_all | solution.py:270
  39.2 17.6 %copy-start.1 = (bf16[144,1024]{1,0:T(8,128)(2,1)}, bf16[144,1024]{1,0:T(8,128)(2,1)S(1)}, u32[]{:S(2)}) copy-start(bf16[144,1024]{1,0:T(8,128)(2,1)S(1)} %shard_map.181.weight.same) | copy-start | bytes 884740
  39.2 17.6 %collective-permute-start.2 = (bf16[8,72,128]{2,1,0:T(8,128)(2,1)S(1)}, bf16[8,72,128]{2,1,0:T(8,128)(2,1)S(1)}, u32[]{:S(2)}, u32[]{:S(2)}) collective-permute-start(bf16[8,72,128]{2,1,0:T(8,128)(2,1)S(1)} %get-tuple-element.33.step), channel_id=1, source_target_pairs={{0,256},{64,320},{128,384},{192,448},{256,0},{320,64},{384,128},{4... | collective-permute-start | bytes 442376 | tf_op jit(solution)/shard_map/ppermute | solution.py:223
  46.1 28.1 %collective-permute-start.3 = (bf16[144,1024]{1,0:T(8,128)(2,1)S(1)}, bf16[144,1024]{1,0:T(8,128)(2,1)S(1)}, u32[]{:S(2)}, u32[]{:S(2)}) collective-permute-start(bf16[144,1024]{1,0:T(8,128)(2,1)S(1)} %shard_map.181.weight.same), channel_id=1, source_target_pairs={{0,4},{4,8},{8,12},{12,0},{1,5},{5,9},{9,13},{13,1},{2,6},{6,10},{... | collective-permute-start | bytes 884744 | tf_op jit(solution)/shard_map/ppermute | solution.py:215
  49.5 24.8 %collective-permute-start.4 = (bf16[144,1024]{1,0:T(8,128)(2,1)S(1)}, bf16[144,1024]{1,0:T(8,128)(2,1)S(1)}, u32[]{:S(2)}, u32[]{:S(2)}) collective-permute-start(bf16[144,1024]{1,0:T(8,128)(2,1)S(1)} %shard_map.181.weight.same), channel_id=1, source_target_pairs={{0,12},{4,0},{8,4},{12,8},{1,13},{5,1},{9,5},{13,9},{2,14},{6,2},{... | collective-permute-start | bytes 884744 | tf_op jit(solution)/shard_map/ppermute | solution.py:215
  51.9 22.3 %collective-permute-start.5 = (bf16[144,1024]{1,0:T(8,128)(2,1)S(1)}, bf16[144,1024]{1,0:T(8,128)(2,1)}, u32[]{:S(2)}, u32[]{:S(2)}) collective-permute-start(bf16[144,1024]{1,0:T(8,128)(2,1)S(1)} %shard_map.181.weight.same), channel_id=1, source_target_pairs={{0,8},{4,12},{8,0},{12,4},{1,9},{5,13},{9,1},{13,5},{2,10},{6,14},... | collective-permute-start | bytes 884744 | tf_op jit(solution)/shard_map/ppermute | solution.py:215
  60.0 14.3 %collective-permute-start.6 = (bf16[8,72,128]{2,1,0:T(8,128)(2,1)}, bf16[8,72,128]{2,1,0:T(8,128)(2,1)S(1)}, u32[]{:S(2)}, u32[]{:S(2)}) collective-permute-start(bf16[8,72,128]{2,1,0:T(8,128)(2,1)} %get-tuple-element.35.step), channel_id=1, source_target_pairs={{0,128},{64,192},{128,0},{192,64},{256,384},{320,448},{384,256},{4... | collective-permute-start | bytes 442376 | tf_op jit(solution)/shard_map/ppermute | solution.py:223
  64.2 23.9 %collective-permute-start.10 = (bf16[72,1152]{1,0:T(8,128)(2,1)}, bf16[72,1152]{1,0:T(8,128)(2,1)S(1)}, u32[]{:S(2)}, u32[]{:S(2)}) collective-permute-start(bf16[72,1152]{1,0:T(8,128)(2,1)} %get-tuple-element.34.done), channel_id=1, source_target_pairs={{0,16},{16,0},{1,17},{17,1},{2,18},{18,2},{3,19},{19,3},{4,20},{20... | collective-permute-start | bytes 497672 | tf_op jit(solution)/shard_map/ppermute | solution.py:211
  75.1 13.1 %copy-start.6 = (f32[1,72,1024]{2,1,0:T(8,128)S(1)}, f32[1,72,1024]{2,1,0:T(8,128)}, u32[]{:S(2)}) copy-start(f32[1,72,1024]{2,1,0:T(8,128)} %param.14) | copy-start | bytes 884740
  75.1 13.1 %copy-start.7 = (f32[1,72,1024]{2,1,0:T(8,128)S(1)}, f32[1,72,1024]{2,1,0:T(8,128)}, u32[]{:S(2)}) copy-start(f32[1,72,1024]{2,1,0:T(8,128)} %param.15) | copy-start | bytes 884740
  75.1 13.1 %copy-start.8 = (f32[72,1024]{1,0:T(8,128)S(1)}, f32[72,1024]{1,0:T(8,128)}, u32[]{:S(2)}) copy-start(f32[72,1024]{1,0:T(8,128)} %get-tuple-element.40.own) | copy-start | bytes 884740
  75.1 13.1 %copy-start.11 = (f32[72,128]{1,0:T(8,128)S(1)}, f32[72,128]{1,0:T(8,128)}, u32[]{:S(2)}) copy-start(f32[72,128]{1,0:T(8,128)} %get-tuple-element.41.gain_own) | copy-start | bytes 110596
  79.1 28.7 %copy-start.19 = (bf16[128,1024]{1,0:T(8,128)(2,1)S(1)}, bf16[128,1024]{1,0:T(8,128)(2,1)}, u32[]{:S(2)}) copy-start(bf16[128,1024]{1,0:T(8,128)(2,1)} %get-tuple-element.39) | copy-start | bytes 786436
  79.1 32.6 %copy-start.5 = (f32[8,72,128]{2,1,0:T(8,128)S(1)}, f32[8,72,128]{2,1,0:T(8,128)}, u32[]{:S(2)}) copy-start(f32[8,72,128]{2,1,0:T(8,128)} %get-tuple-element.46.step) | copy-start | bytes 884740
  79.1 34.6 %copy-start.16 = (f32[1,2304]{1,0:T(1,128)S(1)}, f32[1,2304]{1,0:T(1,128)}, u32[]{:S(2)}) copy-start(f32[1,2304]{1,0:T(1,128)} %gain.1) | copy-start | bytes 27652
  79.1 34.6 %copy-start.17 = (f32[1,2304]{1,0:T(1,128)S(1)}, f32[1,2304]{1,0:T(1,128)}, u32[]{:S(2)}) copy-start(f32[1,2304]{1,0:T(1,128)} %param.18) | copy-start | bytes 27652
  79.1 34.6 %copy-start.18 = (f32[1,2304]{1,0:T(1,128)S(1)}, f32[1,2304]{1,0:T(1,128)}, u32[]{:S(2)}) copy-start(f32[1,2304]{1,0:T(1,128)} %param.17) | copy-start | bytes 27652
  79.1 38.5 %copy-start.3 = (f32[128,1024]{1,0:T(8,128)S(1)}, f32[128,1024]{1,0:T(8,128)}, u32[]{:S(2)}) copy-start(f32[128,1024]{1,0:T(8,128)} %get-tuple-element.36.own) | copy-start | bytes 1572868
  79.1 32.5 %collective-permute-start.11 = (f32[8,72,128]{2,1,0:T(8,128)}, f32[8,72,128]{2,1,0:T(8,128)S(1)}, u32[]{:S(2)}, u32[]{:S(2)}) collective-permute-start(f32[8,72,128]{2,1,0:T(8,128)} %get-tuple-element.46.step), channel_id=1, source_target_pairs={{0,64},{64,0},{128,192},{192,128},{256,320},{320,256},{384,448},{4... | collective-permute-start | bytes 884744 | tf_op jit(solution)/shard_map/ppermute | solution.py:223
  89.3 22.2 %all-to-all-start.2 = ((f32[16,8,128]{2,1,0:T(8,128)}), f32[16,8,128]{2,1,0:T(8,128)S(1)}, u32[]{:S(2)}, u32[]{:S(2)}) async-start(f32[16,8,128]{2,1,0:T(8,128)} %get-tuple-element.45), calls=%async_computation.2 | async-start | bytes 131072 | tf_op jit(solution)/shard_map/all_to_all | solution.py:303
  100.8 13.6 %collective-permute-start.7 = (bf16[128,1024]{1,0:T(8,128)(2,1)}, bf16[128,1024]{1,0:T(8,128)(2,1)S(1)}, u32[]{:S(2)}, u32[]{:S(2)}) collective-permute-start(bf16[128,1024]{1,0:T(8,128)(2,1)} %get-tuple-element.37.after), channel_id=1, source_target_pairs={{0,1},{1,2},{2,3},{3,0},{4,5},{5,6},{6,7},{7,4},{8,9},{9,10},{10,1... | collective-permute-start | bytes 786440 | tf_op jit(solution)/shard_map/ppermute | solution.py:215
  104.1 10.3 %collective-permute-start.8 = (bf16[128,1024]{1,0:T(8,128)(2,1)}, bf16[128,1024]{1,0:T(8,128)(2,1)S(1)}, u32[]{:S(2)}, u32[]{:S(2)}) collective-permute-start(bf16[128,1024]{1,0:T(8,128)(2,1)} %get-tuple-element.38), channel_id=1, source_target_pairs={{0,3},{1,0},{2,1},{3,2},{4,7},{5,4},{6,5},{7,6},{8,11},{9,8},{10,9... | collective-permute-start | bytes 786440 | tf_op jit(solution)/shard_map/ppermute | solution.py:215
  107.8 9.8 %collective-permute-start.9 = (bf16[128,1024]{1,0:T(8,128)(2,1)S(1)}, bf16[128,1024]{1,0:T(8,128)(2,1)S(1)}, u32[]{:S(2)}, u32[]{:S(2)}) collective-permute-start(bf16[128,1024]{1,0:T(8,128)(2,1)S(1)} %copy-done.19), channel_id=1, source_target_pairs={{0,2},{1,3},{2,0},{3,1},{4,6},{5,7},{6,4},{7,5},{8,10},{9,11},{10,... | collective-permute-start | bytes 786440 | tf_op jit(solution)/shard_map/ppermute | solution.py:215
  111.8 7.3 %collective-permute-start.12 = (f32[8,72,128]{2,1,0:T(8,128)S(1)}, f32[8,72,128]{2,1,0:T(8,128)S(1)}, u32[]{:S(2)}, u32[]{:S(2)}) collective-permute-start(f32[8,72,128]{2,1,0:T(8,128)S(1)} %get-tuple-element.49.mine), channel_id=1, source_target_pairs={{0,32},{32,0},{1,33},{33,1},{2,34},{34,2},{3,35},{35,3},{4,36},{36... | collective-permute-start | bytes 884744 | tf_op jit(solution)/shard_map/ppermute | solution.py:211
  (4 other events, 3.0 us)
